TPU v7x, 512 devices: a whole 4x8x8 slice. The times are simulated.
512 devices in a mesh: img: 32 (over z_hi, y, core), txt: 16 (over z_lo, x).
Axes of the slice: x: 4, y: 8, z: 8 (z_hi: 2, z_lo: 4; z = z_hi * 4 + z_lo), core: 2. Of those that a mesh axis runs over, the one named last changes fastest.
Arguments:
- image_features: bfloat16 [4096, 1536], P('img', 'txt'), may hold values from -6 to 6
- text_features: bfloat16 [4096, 1152], P('img', 'txt'), may hold values from -6 to 6
- image_weight: bfloat16 [1536, 1152], P('txt'), may hold values from -0.15625 to 0.15625
- text_weight: bfloat16 [1152, 1152], P('txt'), may hold values from -0.1875 to 0.1875
- pair_index: int32 [4096], P('img'), may hold values from 0 to 4095, each once
Outputs:
- grad_image_weight: float32 [1536, 1152], P('txt')
- grad_text_weight: float32 [1152, 1152], P('txt')
Inputs may be any that keep to these rules, and one draw needn't show every extreme that they name: `pair_index`: every text is the pair of exactly one image.
All inputs are finite; a program needn't handle non-finite values.
Results may differ from a plain program's by a relative error of at most 0.023.
Values may be sent and summed in bfloat16 or wider, within the bound.
No kernel may reach another device: no remote copies, remote signals or barrier semaphores. Data moves between devices by JAX's collectives and lax.ppermute only.
A program may use at most 64 MiB of HBM per device.

v0:
```python
import jax
import jax.numpy as jnp
from jax import lax
from jax.sharding import PartitionSpec as P

LOGIT_SCALE = 10.0
LOGIT_BIAS = -5.0
eps = 1e-06


def passed_along(value, axis, by):
    size = lax.axis_size(axis)
    return lax.ppermute(value, axis, [(i, (i + by) % size) for i in range(size)])


def normalize(pre_values):
    scale = lax.rsqrt(jnp.sum(pre_values * pre_values, -1, keepdims=True) + eps)
    return (pre_values * scale, scale)


def backnorm(unit, scale, upstream):
    along = jnp.sum(unit * upstream, -1, keepdims=True)
    return (upstream - unit * along) * scale


def local(image_features, text_features, image_weight, text_weight, pair_index):
    img_count = lax.axis_size("img")
    txt_count = lax.axis_size("txt")
    img_index = lax.axis_index("img")
    txt_index = lax.axis_index("txt")
    block_rows = image_features.shape[0]
    own_rows = block_rows // txt_count
    embed_width = image_weight.shape[1]
    text_unit, text_scale = normalize(
        lax.psum_scatter(
            jnp.dot(text_features, text_weight, preferred_element_type=jnp.float32).astype(
                jnp.bfloat16
            ),
            "txt",
            scatter_dimension=0,
            tiled=True,
        ).astype(jnp.float32)
    )
    own_text = text_unit.astype(jnp.bfloat16)
    head_terms = jnp.dot(image_features, image_weight, preferred_element_type=jnp.float32)
    image_unit, image_scale = normalize(
        lax.psum(head_terms.astype(jnp.bfloat16), "txt").astype(jnp.float32)
    )
    image_emb = image_unit.astype(jnp.bfloat16)
    col_base = txt_index * own_rows

    def contribute(text_block, anchor):
        col_ids = anchor * block_rows + col_base + jnp.arange(text_block.shape[0], dtype=jnp.int32)
        scores = lax.dot_general(
            text_block, image_emb, (((1,), (1,)), ((), ())), preferred_element_type=jnp.float32
        )
        logits = LOGIT_SCALE * scores + LOGIT_BIAS
        label_sign = jnp.where(col_ids[:, None] == pair_index[None, :], 1.0, -1.0).astype(
            jnp.float32
        )
        pair_grad = (-label_sign * jax.nn.sigmoid(-label_sign * logits)).astype(jnp.bfloat16)
        text_part = LOGIT_SCALE * jnp.dot(pair_grad, image_emb, preferred_element_type=jnp.float32)
        return (pair_grad, text_part)

    seen_texts = jnp.zeros((img_count * own_rows, embed_width), jnp.bfloat16)
    seen_grads = jnp.zeros((img_count * own_rows, block_rows), jnp.bfloat16)

    def cycle_step(turn_index, state_carry):
        text_block, carried, texts_kept, grads_kept = state_carry
        anchor = (img_index - turn_index) % img_count
        pair_grad, text_part = contribute(text_block, anchor)
        texts_kept = lax.dynamic_update_slice_in_dim(
            texts_kept, text_block, turn_index * own_rows, 0
        )
        grads_kept = lax.dynamic_update_slice_in_dim(
            grads_kept, pair_grad, turn_index * own_rows, 0
        )
        text_block = passed_along(text_block, "img", 1)
        carried = passed_along(carried + text_part, "img", 1)
        return (text_block, carried, texts_kept, grads_kept)

    start_state = (
        own_text,
        jnp.zeros((own_rows, embed_width), jnp.float32),
        seen_texts,
        seen_grads,
    )
    final_state = lax.fori_loop(0, img_count, cycle_step, start_state)
    text_grad = final_state[1]
    texts_kept = final_state[2]
    grads_kept = final_state[3]
    contract = (((0,), (0,)), ((), ()))
    image_grad = LOGIT_SCALE * lax.dot_general(
        grads_kept, texts_kept, contract, preferred_element_type=jnp.float32
    )
    text_dpre = backnorm(text_unit, text_scale, text_grad)
    image_total = lax.psum(image_grad, "txt")
    image_dpre = backnorm(image_unit, image_scale, image_total)
    text_dpre_block = lax.all_gather(text_dpre, "txt", axis=0, tiled=True)
    image_local = lax.dot_general(
        image_features.astype(jnp.float32),
        image_dpre,
        contract,
        precision=lax.Precision.HIGHEST,
        preferred_element_type=jnp.float32,
    )
    text_local = lax.dot_general(
        text_features.astype(jnp.float32),
        text_dpre_block,
        contract,
        precision=lax.Precision.HIGHEST,
        preferred_element_type=jnp.float32,
    )
    grad_image_weight, grad_text_weight = lax.psum((image_local, text_local), "img")
    return (grad_image_weight, grad_text_weight)


def solution(mesh):
    in_specs = (P("img", "txt"), P("img", "txt"), P("txt", None), P("txt", None), P("img"))
    out_specs = (P("txt", None), P("txt", None))
    return jax.shard_map(local, mesh=mesh, in_specs=in_specs, out_specs=out_specs, check_vma=False)
```

profile of v0, /device:TPU:1, one launch (start us, length us, event | category | flops | bytes accessed | tf_op | source)
XLA Modules:
  0.0 1143.5 jit_solution(4332493507781482329)
XLA Ops:
  12.9 161.4 %all-reduce.11.cloned.1.call-done = (bf16[128,1152]{1,0:T(8,128)(2,1)}, bf16[128,1152]{1,0:T(8,128)(2,1)}) async-done(((bf16[128,1152]{1,0:T(8,128)(2,1)}, bf16[128,1152]{1,0:T(8,128)(2,1)}), (bf16[128,1152]{1,0:T(8,128)(2,1)}, bf16[128,1152]{1,0:T(8,128)(2,1)})) %all-reduce.11.cloned.1.call-update) | async-done | bytes 589840
  177.9 440.1 %while.21 = (s32[]{:T(128)}, bf16[8,1152]{1,0:T(8,128)(2,1)S(1)}, f32[8,1152]{1,0:T(8,128)S(1)}, bf16[256,1152]{1,0:T(8,128)(2,1)S(1)}, bf16[256,128]{1,0:T(8,12...) while((s32[]{:T(128)}, bf16[8,1152]{1,0:T(8,128)(2,1)S(1)}, ...), condition=%wide.region_5.6_spmd, body=%wide.region_4.5_spmd.sunk | while | flops 4748316 | bytes 984528 | solution.py:88
  177.9 14.6 %collective-permute-start = (bf16[8,1152]{1,0:T(8,128)(2,1)S(1)}, bf16[8,1152]{1,0:T(8,128)(2,1)S(1)}, u32[]{:S(2)}, u32[]{:S(2)}) collective-permute-start(bf16[8,1152]{1,0:T(8,128)(2,1)S(1)} %copy.17), channel_id=1, source_target_pairs={{0,16},{16,32},{32,48},{48,64},{64,80},{80,96},{96,112},{112,128},... | collective-permute-start | bytes 55304 | tf_op jit(solution)/shard_map/while/body/eval_jaxpr/ppermute | solution.py:13
  212.5 6.9 collective-permute-done
  226.1 6.9 collective-permute-done
  239.8 6.9 collective-permute-done
  253.5 6.9 collective-permute-done
  267.1 6.9 collective-permute-done
  280.8 6.9 collective-permute-done
  294.4 6.9 collective-permute-done
  308.1 6.9 collective-permute-done
  321.8 6.9 collective-permute-done
  335.4 6.9 collective-permute-done
  349.1 6.9 collective-permute-done
  362.7 6.9 collective-permute-done
  376.4 6.9 collective-permute-done
  390.1 6.9 collective-permute-done
  403.7 6.9 collective-permute-done
  417.4 6.9 collective-permute-done
  444.7 6.9 collective-permute-done
  458.4 6.9 collective-permute-done
  620.9 34.0 %all_gather.3 = f32[128,1152]{1,0:T(8,128)S(1)} all-gather(f32[8,1152]{1,0:T(8,128)S(1)} %fusion.24), channel_id=1, replica_groups=mesh['img'=32,'txt'=16] {'txt'}, dimensions={0}, use_global_device_ids=true | all-gather | bytes 626688 | tf_op jit(solution)/shard_map/all_gather | solution.py:99
  656.0 124.2 %all-reduce.7.cloned.1.call-done = f32[128,1152]{1,0:T(8,128)} async-done(((f32[128,1152]{1,0:T(8,128)}), f32[128,1152]{1,0:T(8,128)}) %all-reduce.7.cloned.1.call-update) | async-done | bytes 589840 | tf_op jit(solution)/shard_map/psum | solution.py:97
  782.9 351.4 %all-reduce.9.cloned.1.call-done = (f32[96,1152]{1,0:T(8,128)}, f32[72,1152]{1,0:T(8,128)}) async-done(((f32[96,1152]{1,0:T(8,128)}, f32[72,1152]{1,0:T(8,128)}), (f32[96,1152]{1,0:T(8,128)}, f32[72,1152]{1,0:T(8,128)})) %all-reduce.9.cloned.1.call-update) | async-done | bytes 774160 | tf_op jit(solution)/shard_map/psum | solution.py:114
  (311 shorter events, 315.8 us)
Async XLA Ops:
  7.2 167.1 %all-reduce.11.cloned.1.call-start = ((), (), s32[]{:S(2)}) async-start(), calls=%async_computation.2 | async-start | bytes 1179648
  10.8 769.4 %all-reduce.7.cloned.1.call-start = ((), (), s32[]{:S(2)}) async-start(), calls=%async_computation | async-start | bytes 1179648 | tf_op jit(solution)/shard_map/psum | solution.py:97
  177.9 17.0 %collective-permute-start = (bf16[8,1152]{1,0:T(8,128)(2,1)S(1)}, bf16[8,1152]{1,0:T(8,128)(2,1)S(1)}, u32[]{:S(2)}, u32[]{:S(2)}) collective-permute-start(bf16[8,1152]{1,0:T(8,128)(2,1)S(1)} %copy.17), channel_id=1, source_target_pairs={{0,16},{16,32},{32,48},{48,64},{64,80},{80,96},{96,112},{112,128},... | collective-permute-start | bytes 55304 | tf_op jit(solution)/shard_map/while/body/eval_jaxpr/ppermute | solution.py:13
  210.5 11.3 collective-permute-start.1
  224.2 11.3 collective-permute-start.1
  237.8 11.3 collective-permute-start.1
  251.5 11.3 collective-permute-start.1
  265.2 11.3 collective-permute-start.1
  278.8 11.3 collective-permute-start.1
  292.5 11.3 collective-permute-start.1
  306.1 11.3 collective-permute-start.1
  319.8 11.3 collective-permute-start.1
  333.5 11.3 collective-permute-start.1
  347.1 11.3 collective-permute-start.1
  360.8 11.3 collective-permute-start.1
  374.5 11.3 collective-permute-start.1
  388.1 11.3 collective-permute-start.1
  401.8 11.3 collective-permute-start.1
  415.4 11.3 collective-permute-start.1
  429.1 11.3 collective-permute-start.1
  470.1 11.3 collective-permute-start.1
  524.7 11.3 collective-permute-start.1
  579.4 11.3 collective-permute-start.1
  619.1 515.2 %all-reduce.9.cloned.1.call-start = ((), (), s32[]{:S(2)}) async-start(), calls=%async_computation.1 | async-start | bytes 1548288 | tf_op jit(solution)/shard_map/psum | solution.py:114
  (51 other events, 609.4 us)
Sparse Core Ops, SparseCore 0:
  11.6 162.6 all-reduce.10
  619.3 160.8 all-reduce.6
  783.8 350.5 all-reduce.8
where the time goes:
time: 1150 us; the launch traced here: 1140 us
  waiting for transfers between devices  924 us (80%)
  starting transfers between devices  138 us (12%)
  blocking collectives  34 us (3%)
  matrix products  18.5 us (2%)
  between operations  14.5 us (1%)
    psum x1, waiting for transfers between devices, local(): lax.psum((image_local, text_local), 'img')  351 us
    ppermute x64, waiting for transfers between devices, passed_along(): lax.ppermute(value, axis, [(i, (i + by) % size) for i in range(size)])  287 us
    unnamed x4, waiting for transfers between devices  161 us
    ppermute x64, starting transfers between devices, passed_along(): lax.ppermute(value, axis, [(i, (i + by) % size) for i in range(size)])  137 us
    psum x1, waiting for transfers between devices, local(): image_total = lax.psum(image_grad, 'txt')  124 us
    all_gather x1, blocking collectives, local(): text_dpre_block = lax.all_gather(text_dpre, 'txt', axis=0, tiled=True)  34 us
  transfers between devices with their start and end apart: 67, of which 66 were waited for; matrix products, arithmetic and copies ran while one was open for 1% of the time, Pallas kernels for 0%

commit v1 on v0

v1 whole, which is shorter than its diff:
```python
import jax
import jax.numpy as jnp
import numpy as np
from jax import lax
from jax.sharding import Mesh
from jax.sharding import PartitionSpec as P

LOGIT_SCALE = 10.0
LOGIT_BIAS = -5.0
EPS = 1e-06
E = 1152
LANES = 128
WIDE = 2 * E + LANES
AXES = ("zh", "y", "core", "zl", "x")
IMG = ("zh", "y", "core")
ZY = ("zh", "y")
TXT = ("zl", "x")
bf16 = jnp.bfloat16
f32 = jnp.float32


def exchange(value, axis):
    return lax.all_to_all(value, axis, 0, 0, tiled=True)


def head_partials(image_features, text_features, image_weight, text_weight):
    image = jnp.dot(image_features, image_weight, preferred_element_type=f32)
    text = jnp.dot(text_features, text_weight, preferred_element_type=f32)
    return jnp.concatenate([image.astype(bf16), text.astype(bf16)], axis=1)


def split_hi_lo(value):
    hi = value.astype(bf16).astype(f32)
    return hi, value - hi


def unit_rows(partials, own_pairs, copies):
    rows = partials.shape[0] // 16
    total = jnp.sum(partials.astype(f32).reshape(16, rows, 2 * E), axis=0)
    pieces = []
    scales = []
    for tower in range(2):
        pre = total[:, tower * E : (tower + 1) * E]
        scale = lax.rsqrt(jnp.sum(pre * pre, -1, keepdims=True) + EPS)
        pieces.append(pre * scale)
        scales.append(scale)
    lane = lax.broadcasted_iota(jnp.int32, (rows, LANES), 1)
    pair_hi = jnp.floor(own_pairs * (1.0 / 64.0))
    pair_lo = own_pairs - 64.0 * pair_hi
    extra = jnp.zeros((rows, LANES), f32)
    columns = [pair_hi, pair_lo, *split_hi_lo(scales[0]), *split_hi_lo(scales[1])]
    for place, column in enumerate(columns):
        extra = jnp.where(lane == place, column, extra)
    row_block = jnp.concatenate(pieces + [extra], axis=1)
    return jnp.tile(row_block, (copies, 1)).astype(bf16)


def grad_terms(n1, n2_blocks, n1_ids_base, n2_ids_bases, n1_count):
    rows = n1.shape[0]
    info = n1[:, 2 * E :].astype(f32)
    n1_pairs = info[:, 0:1] * 64.0 + info[:, 1:2]
    scales = [info[:, 2:3] + info[:, 3:4], info[:, 4:5] + info[:, 5:6]]
    nt = (((1,), (1,)), ((), ()))
    tn = (((0,), (0,)), ((), ()))
    image_grad = jnp.zeros((rows, E), f32)
    text_grad = jnp.zeros((rows, E), f32)
    image1 = n1[:, :E]
    text1 = n1[:, E : 2 * E]
    for block, base in zip(n2_blocks, n2_ids_bases):
        image2 = block[:, :E]
        text2 = block[:, E : 2 * E]
        count = block.shape[0]
        logits = LOGIT_SCALE * lax.dot_general(image1, text2, nt, preferred_element_type=f32) + LOGIT_BIAS
        ids = (base + lax.broadcasted_iota(jnp.int32, (rows, count), 1)).astype(f32)
        label = jnp.where(ids == n1_pairs, 1.0, 0.0)
        pair_grad = (1.0 / (1.0 + jnp.exp(-logits)) - label).astype(bf16)
        image_grad = image_grad + jnp.dot(pair_grad, text2, preferred_element_type=f32)
        logits = LOGIT_SCALE * lax.dot_general(image2, text1, nt, preferred_element_type=f32) + LOGIT_BIAS
        info2 = block[:, 2 * E :].astype(f32)
        n2_pairs = info2[:, 0:1] * 64.0 + info2[:, 1:2]
        place = lax.broadcasted_iota(jnp.int32, (count, rows), 1)
        ids = (n1_ids_base + (place // 8) * 256 + place % 8).astype(f32)
        label = jnp.where(ids == n2_pairs, 1.0, 0.0)
        pair_grad = (1.0 / (1.0 + jnp.exp(-logits)) - label).astype(bf16)
        text_grad = text_grad + lax.dot_general(pair_grad, image2, tn, preferred_element_type=f32)
    pieces = []
    for unit, grad, scale in ((image1, image_grad, scales[0]), (text1, text_grad, scales[1])):
        unit = unit.astype(f32)
        along = jnp.sum(unit * grad, -1, keepdims=True)
        pieces.append(((grad - unit * along) * (scale * LOGIT_SCALE)).T)
    return jnp.concatenate(pieces, axis=0).astype(bf16)


def summed(parts, copies):
    rows = parts.shape[0] // 16
    total = jnp.sum(parts.astype(f32).reshape(16, rows, LANES), axis=0)
    return jnp.tile(total, (copies, 1)).astype(bf16)


def local(image_features, text_features, image_weight, text_weight, pair_index):
    zy = lax.axis_index(ZY)
    zh = lax.axis_index("zh")
    core = lax.axis_index("core")
    txt = lax.axis_index(TXT)
    block_rows = image_features.shape[0]
    own_rows = block_rows // 16
    image_cols = image_features.shape[1]
    text_cols = text_features.shape[1]

    lanes = jnp.concatenate(
        [
            jnp.pad(image_features, ((0, 0), (0, LANES - image_cols))),
            jnp.pad(text_features, ((0, 0), (0, LANES - text_cols))),
        ],
        axis=1,
    )
    everyone = lax.all_gather(lanes, IMG, axis=0, tiled=True)

    partials = exchange(head_partials(image_features, text_features, image_weight, text_weight), TXT)
    own_pairs = lax.dynamic_slice_in_dim(pair_index, txt * own_rows, own_rows, 0).astype(f32)[:, None]
    repeated = unit_rows(partials, own_pairs, 16)
    block = exchange(repeated, TXT)
    sibling = lax.ppermute(block, "core", [(0, 1), (1, 0)])
    n1 = exchange(repeated, ZY)
    own_base = (zy * 2 + core) * block_rows
    sibling_base = (zy * 2 + 1 - core) * block_rows
    n1_base = core * block_rows + txt * own_rows
    terms = grad_terms(n1, [block, sibling], n1_base, [own_base, sibling_base], own_rows)
    dpre = exchange(summed(exchange(terms, ZY), 16), TXT)

    ordered = everyone.reshape(16, 2, 16, own_rows, 2, LANES)
    ordered = lax.dynamic_index_in_dim(ordered, core, 1, keepdims=False)
    ordered = lax.dynamic_index_in_dim(ordered, zh, 3, keepdims=False)
    ordered = ordered.transpose(1, 0, 2, 3).reshape(16, 16 * own_rows, LANES)
    dpre = dpre.reshape(16, -1, LANES)
    weight_grad = jnp.zeros((dpre.shape[1], LANES), f32)
    for step in range(16):
        weight_grad = weight_grad + jnp.dot(dpre[step], ordered[step], preferred_element_type=f32)
    both = lax.all_gather(weight_grad, "core", axis=0, tiled=False)
    weight_grad = jnp.sum(both, axis=0).astype(bf16)
    whole = exchange(jnp.tile(weight_grad, (16, 1)), ZY).astype(f32)
    return whole[:E, :image_cols].T, whole[E:, :text_cols].T


def solution(mesh):
    fine = Mesh(mesh.devices.reshape(2, 8, 2, 4, 4), AXES)
    in_specs = (P(IMG, TXT), P(IMG, TXT), P(TXT, None), P(TXT, None), P(IMG))
    out_specs = (P(TXT, None), P(TXT, None))
    return jax.shard_map(local, mesh=fine, in_specs=in_specs, out_specs=out_specs, check_vma=False)
```

time: 1150 us -> 218 us (0.19)
  the two profiles are of different devices: /device:TPU:1 before, /device:TPU:128 now
where the time goes in v1:
time: 218 us; the launch traced here: 217 us
  blocking collectives  82.2 us (38%)
  waiting for transfers between devices  75.2 us (34%)
  starting transfers between devices  29.2 us (13%)
  between operations  14.4 us (7%)
  matrix products  7.18 us (3%)
  local copies, waits for them, and re-layouts  5.48 us (3%)
  other arithmetic  3.23 us (1%)
    all_to_all x3, blocking collectives, exchange(): return lax.all_to_all(value, axis, 0, 0, tiled=True)  80.3 us
    all_gather x1, waiting for transfers between devices, local(): everyone = lax.all_gather(lanes, IMG, axis=0, tiled=True)  42.5 us
    all_to_all x3, waiting for transfers between devices, exchange(): return lax.all_to_all(value, axis, 0, 0, tiled=True)  32.7 us
    all_to_all x3, starting transfers between devices, exchange(): return lax.all_to_all(value, axis, 0, 0, tiled=True)  27.3 us
  transfers between devices with their start and end apart: 5, of which 3 were waited for; matrix products, arithmetic and copies ran while one was open for 3% of the time, Pallas kernels for 0%

profile of v1, /device:TPU:128, one launch (start us, length us, event | category | flops | bytes accessed | tf_op | source)
XLA Modules:
  0.0 216.9 jit_solution(16903913071380930977)
XLA Ops:
  7.2 1.2 convolution_convert_fusion
  8.4 1.0 convolution_convert_fusion.1
  9.5 0.9 maximum_bitcast_fusion
  10.3 8.5 %all-to-all-start = ((bf16[16,8,2304]{2,1,0:T(8,128)(2,1)}), bf16[16,8,2304]{2,1,0:T(8,128)(2,1)S(1)}, u32[]{:S(2)}, u32[]{:S(2)}) async-start(bf16[16,8,2304]{2,1,0:T(8,128)(2,1)} %maximum_bitcast_fusion), calls=%async_computation | async-start | bytes 1179648 | tf_op jit(solution)/shard_map/all_to_all | solution.py:23
  18.9 15.8 %all-to-all-done = bf16[16,8,2304]{2,1,0:T(8,128)(2,1)S(1)} async-done(((bf16[16,8,2304]{2,1,0:T(8,128)(2,1)}), bf16[16,8,2304]{2,1,0:T(8,128)(2,1)S(1)}, u32[]{:S(2)}, u32[]{:S(2)}) %all-to-all-start) | async-done | bytes 589856 | tf_op jit(solution)/shard_map/all_to_all | solution.py:23
  35.1 0.9 tile.6
  36.0 21.2 %all_to_all.45 = bf16[16,8,2432]{2,1,0:T(8,128)(2,1)S(1)} all-to-all(bf16[16,8,2432]{2,1,0:T(8,128)(2,1)} %tile.6), channel_id=1, replica_groups=mesh['zh'=2,'y'=8,'core'=2,'zl'=4,'x'=4] {'zl','x'}, dimensions={0} | all-to-all | bytes 1245184 | tf_op jit(solution)/shard_map/all_to_all | solution.py:23
  57.2 13.0 %all-to-all-start.1 = ((bf16[16,8,2432]{2,1,0:T(8,128)(2,1)}), bf16[16,8,2432]{2,1,0:T(8,128)(2,1)S(1)}, u32[]{:S(2)}, u32[]{:S(2)}) async-start(bf16[16,8,2432]{2,1,0:T(8,128)(2,1)} %tile.6), calls=%async_computation.1 | async-start | bytes 1245184 | tf_op jit(solution)/shard_map/all_to_all | solution.py:23
  70.4 0.7 fusion.58
  71.2 1.9 collective-permute-start
  73.1 16.9 %all-to-all-done.1 = bf16[16,8,2432]{2,1,0:T(8,128)(2,1)S(1)} async-done(((bf16[16,8,2432]{2,1,0:T(8,128)(2,1)}), bf16[16,8,2432]{2,1,0:T(8,128)(2,1)S(1)}, u32[]{:S(2)}, u32[]{:S(2)}) %all-to-all-start.1) | async-done | bytes 622624 | tf_op jit(solution)/shard_map/all_to_all | solution.py:23
  90.5 0.6 fusion.28
  91.1 0.5 fusion.29
  91.9 0.6 convolution_add_fusion
  92.5 0.6 fusion.30
  93.8 28.0 %all_to_all.46 = bf16[16,144,128]{2,1,0:T(8,128)(2,1)S(1)} all-to-all(bf16[16,144,128]{2,1,0:T(8,128)(2,1)S(1)} %bitcast.132), channel_id=1, replica_groups=mesh['zh'=2,'y'=8,'core'=2,'zl'=4,'x'=4] {'zh','y'}, dimensions={0} | all-to-all | bytes 1179648 | tf_op jit(solution)/shard_map/all_to_all | solution.py:23
  121.9 0.9 tile.7
  122.8 5.8 %all-to-all-start.4 = ((bf16[16,144,128]{2,1,0:T(8,128)(2,1)}), bf16[16,144,128]{2,1,0:T(8,128)(2,1)S(1)}, u32[]{:S(2)}, u32[]{:S(2)}) async-start(bf16[16,144,128]{2,1,0:T(8,128)(2,1)} %tile.7), calls=%async_computation.4 | async-start | bytes 1179648 | tf_op jit(solution)/shard_map/all_to_all | solution.py:23
  128.6 42.5 %all-gather.3.cloned.1.call-done = bf16[4096,256]{1,0:T(8,128)(2,1)} async-done(((bf16[128,256]{1,0:T(8,128)(2,1)}), bf16[4096,256]{1,0:T(8,128)(2,1)}) %all-gather.3.cloned.1.call-update) | async-done | bytes 2097168 | tf_op jit(solution)/shard_map/all_gather | solution.py:117
  171.1 1.1 dynamic-slice_bitcast_fusion
  174.8 1.9 all-gather
  176.9 31.1 %all_to_all.47 = bf16[16,144,128]{2,1,0:T(8,128)(2,1)S(1)} all-to-all(bf16[16,144,128]{2,1,0:T(8,128)(2,1)S(1)} %tile.8), channel_id=1, replica_groups=mesh['zh'=2,'y'=8,'core'=2,'zl'=4,'x'=4] {'zh','y'}, dimensions={0} | all-to-all | bytes 1179648 | tf_op jit(solution)/shard_map/all_to_all | solution.py:23
  208.1 1.0 copy.15
  209.1 0.9 copy.16
  (61 shorter events, 5.0 us)
Async XLA Ops:
  7.2 1.3 copy-start
  9.4 9.4 %copy-start.3 = (s32[128]{0:T(128)S(1)}, s32[128]{0:T(128)}, u32[]{:S(2)}) copy-start(s32[128]{0:T(128)} %param.9) | copy-start | bytes 1540
  10.3 24.4 %all-to-all-start = ((bf16[16,8,2304]{2,1,0:T(8,128)(2,1)}), bf16[16,8,2304]{2,1,0:T(8,128)(2,1)S(1)}, u32[]{:S(2)}, u32[]{:S(2)}) async-start(bf16[16,8,2304]{2,1,0:T(8,128)(2,1)} %maximum_bitcast_fusion), calls=%async_computation | async-start | bytes 1179648 | tf_op jit(solution)/shard_map/all_to_all | solution.py:23
  36.0 34.2 %copy-start.1 = (bf16[128,96]{0,1:T(8,128)(2,1)S(1)}, bf16[128,96]{0,1:T(8,128)(2,1)}, u32[]{:S(2)}) copy-start(bf16[128,96]{0,1:T(8,128)(2,1)} %param.5) | copy-start | bytes 73732
  36.0 34.3 %copy-start.2 = (bf16[128,72]{0,1:T(8,128)(2,1)S(1)}, bf16[128,72]{0,1:T(8,128)(2,1)}, u32[]{:S(2)}) copy-start(bf16[128,72]{0,1:T(8,128)(2,1)} %param.6) | copy-start | bytes 55300
  57.2 32.8 %all-to-all-start.1 = ((bf16[16,8,2432]{2,1,0:T(8,128)(2,1)}), bf16[16,8,2432]{2,1,0:T(8,128)(2,1)S(1)}, u32[]{:S(2)}, u32[]{:S(2)}) async-start(bf16[16,8,2432]{2,1,0:T(8,128)(2,1)} %tile.6), calls=%async_computation.1 | async-start | bytes 1245184 | tf_op jit(solution)/shard_map/all_to_all | solution.py:23
  70.1 101.0 %all-gather.3.cloned.1.call-start = ((), (), s32[]{:S(2)}) async-start(), calls=%async_computation.6 | async-start | bytes 2162688 | tf_op jit(solution)/shard_map/all_gather | solution.py:117
  71.2 20.4 %collective-permute-start = (bf16[128,2432]{1,0:T(8,128)(2,1)S(1)}, bf16[128,2432]{1,0:T(8,128)(2,1)S(1)}, u32[]{:S(2)}, u32[]{:S(2)}) collective-permute-start(bf16[128,2432]{1,0:T(8,128)(2,1)S(1)} %bitcast.128), channel_id=1, source_target_pairs={{0,16},{16,0},{1,17},{17,1},{2,18},{18,2},{3,19},{19,3},{4,20},{20... | collective-permute-start | bytes 1867784 | tf_op jit(solution)/shard_map/ppermute | solution.py:123
  122.8 49.5 %all-to-all-start.4 = ((bf16[16,144,128]{2,1,0:T(8,128)(2,1)}), bf16[16,144,128]{2,1,0:T(8,128)(2,1)S(1)}, u32[]{:S(2)}, u32[]{:S(2)}) async-start(bf16[16,144,128]{2,1,0:T(8,128)(2,1)} %tile.7), calls=%async_computation.4 | async-start | bytes 1179648 | tf_op jit(solution)/shard_map/all_to_all | solution.py:23
Sparse Core Ops, SparseCore 0:
  74.9 96.2 all-gather.2

commit v2 on v1

--- a/solution.py
+++ b/solution.py
@@ -99,7 +99,6 @@
 
 def local(image_features, text_features, image_weight, text_weight, pair_index):
     zy = lax.axis_index(ZY)
-    zh = lax.axis_index("zh")
     core = lax.axis_index("core")
     txt = lax.axis_index(TXT)
     block_rows = image_features.shape[0]
@@ -107,35 +106,32 @@
     image_cols = image_features.shape[1]
     text_cols = text_features.shape[1]
 
-    lanes = jnp.concatenate(
-        [
-            jnp.pad(image_features, ((0, 0), (0, LANES - image_cols))),
-            jnp.pad(text_features, ((0, 0), (0, LANES - text_cols))),
-        ],
-        axis=1,
-    )
-    everyone = lax.all_gather(lanes, IMG, axis=0, tiled=True)
+    def by_own_rows(features, cols):
+        padded = jnp.pad(features, ((0, 0), (0, LANES - cols)))
+        return padded.reshape(16, own_rows, LANES).transpose(1, 0, 2).reshape(own_rows, 16 * LANES)
+
+    image_rows = by_own_rows(image_features, image_cols)
+    text_rows = by_own_rows(text_features, text_cols)
+    feature_rows = jnp.concatenate([jnp.tile(image_rows, (8, 1)), jnp.tile(text_rows, (8, 1))], axis=0)
 
     partials = exchange(head_partials(image_features, text_features, image_weight, text_weight), TXT)
     own_pairs = lax.dynamic_slice_in_dim(pair_index, txt * own_rows, own_rows, 0).astype(f32)[:, None]
     repeated = unit_rows(partials, own_pairs, 16)
     block = exchange(repeated, TXT)
     sibling = lax.ppermute(block, "core", [(0, 1), (1, 0)])
-    n1 = exchange(repeated, ZY)
+    received = exchange(jnp.concatenate([repeated, feature_rows], axis=1), ZY)
+    n1 = received[:, :WIDE]
     own_base = (zy * 2 + core) * block_rows
     sibling_base = (zy * 2 + 1 - core) * block_rows
     n1_base = core * block_rows + txt * own_rows
     terms = grad_terms(n1, [block, sibling], n1_base, [own_base, sibling_base], own_rows)
     dpre = exchange(summed(exchange(terms, ZY), 16), TXT)
 
-    ordered = everyone.reshape(16, 2, 16, own_rows, 2, LANES)
-    ordered = lax.dynamic_index_in_dim(ordered, core, 1, keepdims=False)
-    ordered = lax.dynamic_index_in_dim(ordered, zh, 3, keepdims=False)
-    ordered = ordered.transpose(1, 0, 2, 3).reshape(16, 16 * own_rows, LANES)
     dpre = dpre.reshape(16, -1, LANES)
     weight_grad = jnp.zeros((dpre.shape[1], LANES), f32)
     for step in range(16):
-        weight_grad = weight_grad + jnp.dot(dpre[step], ordered[step], preferred_element_type=f32)
+        ordered = received[:, WIDE + step * LANES : WIDE + (step + 1) * LANES]
+        weight_grad = weight_grad + jnp.dot(dpre[step], ordered, preferred_element_type=f32)
     both = lax.all_gather(weight_grad, "core", axis=0, tiled=False)
     weight_grad = jnp.sum(both, axis=0).astype(bf16)
     whole = exchange(jnp.tile(weight_grad, (16, 1)), ZY).astype(f32)

time: 218 us -> 187 us (0.86)
  the two profiles are of different devices: /device:TPU:128 before, /device:TPU:1 now
where the time goes in v2:
time: 187 us; the launch traced here: 185 us
  blocking collectives  83.6 us (45%)
  waiting for transfers between devices  47.1 us (25%)
  starting transfers between devices  34.4 us (18%)
  matrix products  9.69 us (5%)
  other arithmetic  5.82 us (3%)
  local copies, waits for them, and re-layouts  3.7 us (2%)
    all_to_all x3, blocking collectives, exchange(): return lax.all_to_all(value, axis, 0, 0, tiled=True)  77.9 us
    all_to_all x3, waiting for transfers between devices, exchange(): return lax.all_to_all(value, axis, 0, 0, tiled=True)  45.7 us
    all_to_all x3, starting transfers between devices, exchange(): return lax.all_to_all(value, axis, 0, 0, tiled=True)  28.5 us
    ppermute x1, starting transfers between devices, local(): sibling = lax.ppermute(block, 'core', [(0, 1), (1, 0)])  5.9 us
    all_gather x1, blocking collectives, local(): both = lax.all_gather(weight_grad, 'core', axis=0, tiled=False)  5.69 us
  transfers between devices with their start and end apart: 4, of which 4 were waited for; matrix products, arithmetic and copies ran while one was open for 2% of the time, Pallas kernels for 0%

profile of v2, /device:TPU:1, one launch (start us, length us, event | category | flops | bytes accessed | tf_op | source)
XLA Modules:
  0.0 185.3 jit_solution(9569108158677884401)
XLA Ops:
  0.6 1.2 convolution_convert_fusion
  1.9 1.0 convolution_convert_fusion.1
  2.9 0.9 maximum_bitcast_fusion
  3.8 10.4 %all-to-all-start = ((bf16[16,8,2304]{2,1,0:T(8,128)(2,1)}), bf16[16,8,2304]{2,1,0:T(8,128)(2,1)S(1)}, u32[]{:S(2)}, u32[]{:S(2)}) async-start(bf16[16,8,2304]{2,1,0:T(8,128)(2,1)} %maximum_bitcast_fusion), calls=%async_computation | async-start | bytes 1179648 | tf_op jit(solution)/shard_map/all_to_all | solution.py:23
  14.6 14.4 %all-to-all-done = bf16[16,8,2304]{2,1,0:T(8,128)(2,1)S(1)} async-done(((bf16[16,8,2304]{2,1,0:T(8,128)(2,1)}), bf16[16,8,2304]{2,1,0:T(8,128)(2,1)S(1)}, u32[]{:S(2)}, u32[]{:S(2)}) %all-to-all-start) | async-done | bytes 589856 | tf_op jit(solution)/shard_map/all_to_all | solution.py:23
  29.4 0.9 tile.18
  30.4 5.5 %all-to-all-start.2 = ((bf16[16,8,2432]{2,1,0:T(8,128)(2,1)}), bf16[16,8,2432]{2,1,0:T(8,128)(2,1)S(1)}, u32[]{:S(2)}, u32[]{:S(2)}) async-start(bf16[16,8,2432]{2,1,0:T(8,128)(2,1)} %tile.18), calls=%async_computation.2 | async-start | bytes 1245184 | tf_op jit(solution)/shard_map/all_to_all | solution.py:23
  35.9 2.2 %pad_maximum_fusion = bf16[16,8,4480]{2,1,0:T(8,128)(2,1)} fusion(bf16[16,8,2048]{2,1,0:T(8,128)(2,1)S(1)} %maximum_bitcast_fusion.1, bf16[16,8,2432]{2,1,0:T(8,128)(2,1)} %tile.18), kind=kLoop, calls=%fused_computation.5 | loop fusion | flops 2293760 | bytes 2293760 | tf_op jit(solution)/shard_map/concatenate | solution.py:122
  38.1 12.3 %all-to-all-done.2 = bf16[16,8,2432]{2,1,0:T(8,128)(2,1)S(1)} async-done(((bf16[16,8,2432]{2,1,0:T(8,128)(2,1)}), bf16[16,8,2432]{2,1,0:T(8,128)(2,1)S(1)}, u32[]{:S(2)}, u32[]{:S(2)}) %all-to-all-start.2) | async-done | bytes 622624 | tf_op jit(solution)/shard_map/all_to_all | solution.py:23
  50.4 12.7 %all-to-all-start.1 = ((bf16[16,8,4480]{2,1,0:T(8,128)(2,1)}), bf16[16,8,4480]{2,1,0:T(8,128)(2,1)S(1)}, u32[]{:S(2)}, u32[]{:S(2)}) async-start(bf16[16,8,4480]{2,1,0:T(8,128)(2,1)} %pad_maximum_fusion), calls=%async_computation.1 | async-start | bytes 2293760 | tf_op jit(solution)/shard_map/all_to_all | solution.py:23
  63.1 5.9 %collective-permute-start = (bf16[128,2432]{1,0:T(8,128)(2,1)S(1)}, bf16[128,2432]{1,0:T(8,128)(2,1)S(1)}, u32[]{:S(2)}, u32[]{:S(2)}) collective-permute-start(bf16[128,2432]{1,0:T(8,128)(2,1)S(1)} %bitcast.109), channel_id=1, source_target_pairs={{0,16},{16,0},{1,17},{17,1},{2,18},{18,2},{3,19},{19,3},{4,20},{20... | collective-permute-start | bytes 1867784 | tf_op jit(solution)/shard_map/ppermute | solution.py:121
  69.2 1.4 collective-permute-done
  70.8 19.0 %all-to-all-done.1 = bf16[16,8,4480]{2,1,0:T(8,128)(2,1)S(1)} async-done(((bf16[16,8,4480]{2,1,0:T(8,128)(2,1)}), bf16[16,8,4480]{2,1,0:T(8,128)(2,1)S(1)}, u32[]{:S(2)}, u32[]{:S(2)}) %all-to-all-start.1) | async-done | bytes 1146912 | tf_op jit(solution)/shard_map/all_to_all | solution.py:23
  90.1 0.5 fusion.29
  90.7 1.4 fusion.28
  92.1 1.7 convolution_add_fusion
  93.8 1.4 fusion.30
  95.1 1.3 fusion.39
  96.8 25.7 %all_to_all.45 = bf16[16,144,128]{2,1,0:T(8,128)(2,1)S(1)} all-to-all(bf16[16,144,128]{2,1,0:T(8,128)(2,1)S(1)} %bitcast.113), channel_id=1, replica_groups=mesh['zh'=2,'y'=8,'core'=2,'zl'=4,'x'=4] {'zh','y'}, dimensions={0} | all-to-all | bytes 1179648 | tf_op jit(solution)/shard_map/all_to_all | solution.py:23
  122.7 26.0 %all_to_all.46 = bf16[16,144,128]{2,1,0:T(8,128)(2,1)S(1)} all-to-all(bf16[16,144,128]{2,1,0:T(8,128)(2,1)S(1)} %tile.48), channel_id=1, replica_groups=mesh['zh'=2,'y'=8,'core'=2,'zl'=4,'x'=4] {'zl','x'}, dimensions={0} | all-to-all | bytes 1179648 | tf_op jit(solution)/shard_map/all_to_all | solution.py:23
  151.3 5.7 %all-gather = f32[288,128]{1,0:T(8,128)S(1)} all-gather(f32[144,128]{1,0:T(8,128)S(1)} %convolution_add_fusion.2), channel_id=2, replica_groups=mesh['zh'=2,'y'=8,'core'=2,'zl'=4,'x'=4] {'core'}, dimensions={0}, use_global_device_ids=true | all-gather | bytes 221184 | tf_op jit(solution)/shard_map/all_gather | solution.py:135
  157.1 26.1 %all_to_all.47 = bf16[16,144,128]{2,1,0:T(8,128)(2,1)S(1)} all-to-all(bf16[16,144,128]{2,1,0:T(8,128)(2,1)S(1)} %tile.49), channel_id=1, replica_groups=mesh['zh'=2,'y'=8,'core'=2,'zl'=4,'x'=4] {'zh','y'}, dimensions={0} | all-to-all | bytes 1179648 | tf_op jit(solution)/shard_map/all_to_all | solution.py:23
  183.4 1.0 copy.10
  184.4 0.9 copy.11
  (61 shorter events, 4.8 us)
Async XLA Ops:
  0.6 1.3 copy-start
  2.9 11.3 %copy-start.2 = (bf16[128,72]{0,1:T(8,128)(2,1)S(1)}, bf16[128,72]{0,1:T(8,128)(2,1)}, u32[]{:S(2)}) copy-start(bf16[128,72]{0,1:T(8,128)(2,1)} %param.6) | copy-start | bytes 55300
  2.9 11.4 %copy-start.1 = (bf16[128,96]{0,1:T(8,128)(2,1)S(1)}, bf16[128,96]{0,1:T(8,128)(2,1)}, u32[]{:S(2)}) copy-start(bf16[128,96]{0,1:T(8,128)(2,1)} %param.5) | copy-start | bytes 73732
  2.9 11.6 %copy-start.3 = (s32[128]{0:T(128)S(1)}, s32[128]{0:T(128)}, u32[]{:S(2)}) copy-start(s32[128]{0:T(128)} %param.9) | copy-start | bytes 1540
  3.8 25.2 %all-to-all-start = ((bf16[16,8,2304]{2,1,0:T(8,128)(2,1)}), bf16[16,8,2304]{2,1,0:T(8,128)(2,1)S(1)}, u32[]{:S(2)}, u32[]{:S(2)}) async-start(bf16[16,8,2304]{2,1,0:T(8,128)(2,1)} %maximum_bitcast_fusion), calls=%async_computation | async-start | bytes 1179648 | tf_op jit(solution)/shard_map/all_to_all | solution.py:23
  30.4 20.0 %all-to-all-start.2 = ((bf16[16,8,2432]{2,1,0:T(8,128)(2,1)}), bf16[16,8,2432]{2,1,0:T(8,128)(2,1)S(1)}, u32[]{:S(2)}, u32[]{:S(2)}) async-start(bf16[16,8,2432]{2,1,0:T(8,128)(2,1)} %tile.18), calls=%async_computation.2 | async-start | bytes 1245184 | tf_op jit(solution)/shard_map/all_to_all | solution.py:23
  50.4 39.5 %all-to-all-start.1 = ((bf16[16,8,4480]{2,1,0:T(8,128)(2,1)}), bf16[16,8,4480]{2,1,0:T(8,128)(2,1)S(1)}, u32[]{:S(2)}, u32[]{:S(2)}) async-start(bf16[16,8,4480]{2,1,0:T(8,128)(2,1)} %pad_maximum_fusion), calls=%async_computation.1 | async-start | bytes 2293760 | tf_op jit(solution)/shard_map/all_to_all | solution.py:23
  63.1 7.6 %collective-permute-start = (bf16[128,2432]{1,0:T(8,128)(2,1)S(1)}, bf16[128,2432]{1,0:T(8,128)(2,1)S(1)}, u32[]{:S(2)}, u32[]{:S(2)}) collective-permute-start(bf16[128,2432]{1,0:T(8,128)(2,1)S(1)} %bitcast.109), channel_id=1, source_target_pairs={{0,16},{16,0},{1,17},{17,1},{2,18},{18,2},{3,19},{19,3},{4,20},{20... | collective-permute-start | bytes 1867784 | tf_op jit(solution)/shard_map/ppermute | solution.py:121

commit v3 on v2

v3 whole, which is shorter than its diff:
```python
import jax
import jax.numpy as jnp
from jax import lax
from jax.sharding import Mesh
from jax.sharding import PartitionSpec as P

LOGIT_SCALE = 10.0
LOGIT_BIAS = -5.0
EPS = 1e-06
E = 1152
LANES = 128
AXES = ("zh", "y", "core", "zl", "x")
IMG = ("zh", "y", "core")
ZY = ("zh", "y")
TXT = ("zl", "x")
bf16 = jnp.bfloat16
f32 = jnp.float32


def exchange(value, axis):
    return lax.all_to_all(value, axis, 0, 0, tiled=True)


def swap(value, axis):
    return lax.ppermute(value, axis, [(0, 1), (1, 0)])


def head_partials(image_features, text_features, image_weight, text_weight):
    image = jnp.dot(image_features, image_weight, preferred_element_type=f32)
    text = jnp.dot(text_features, text_weight, preferred_element_type=f32)
    return jnp.concatenate([image.astype(bf16), text.astype(bf16)], axis=1)


def columns_in_lanes(columns, rows):
    lane = lax.broadcasted_iota(jnp.int32, (rows, LANES), 1)
    lanes = jnp.zeros((rows, LANES), f32)
    for place, column in enumerate(columns):
        lanes = jnp.where(lane == place, column, lanes)
    return lanes


def key_digits(key):
    hi = jnp.floor(key * (1.0 / 64.0))
    return [hi, key - 64.0 * hi]


def hi_lo(value):
    hi = value.astype(bf16).astype(f32)
    return [hi, value - hi]


def unit_rows(partials, pairs, ids):
    rows = partials.shape[0] // 16
    total = jnp.sum(partials.astype(f32).reshape(16, rows, 2 * E), axis=0)
    first, second = [], []
    for tower, (key1, key2) in enumerate(((pairs, pairs), (ids, ids))):
        pre = total[:, tower * E : (tower + 1) * E]
        scale = lax.rsqrt(jnp.sum(pre * pre, -1, keepdims=True) + EPS)
        unit = pre * scale
        extra1 = columns_in_lanes(key_digits(key1) + hi_lo(scale), rows)
        extra2 = columns_in_lanes(key_digits(key2), rows)
        first.append(jnp.concatenate([unit, extra1], axis=1).astype(bf16))
        second.append(jnp.concatenate([unit, extra2], axis=1).astype(bf16))
    return first, second


def grad_terms(n1, n2_blocks):
    rows = n1.shape[0]
    info = n1[:, E : E + LANES].astype(f32)
    key1 = info[:, 0:1] * 64.0 + info[:, 1:2]
    scale = info[:, 2:3] + info[:, 3:4]
    unit = n1[:, :E]
    grad = jnp.zeros((rows, E), f32)
    for block in n2_blocks:
        other = block[:, :E]
        info2 = block[:, E:].astype(f32).T
        key2 = info2[0:1] * 64.0 + info2[1:2]
        scores = lax.dot_general(unit, other, (((1,), (1,)), ((), ())), preferred_element_type=f32)
        logits = LOGIT_SCALE * scores + LOGIT_BIAS
        label = jnp.where(key1 == key2, 1.0, 0.0)
        pair_grad = (1.0 / (1.0 + jnp.exp(-logits)) - label).astype(bf16)
        grad = grad + jnp.dot(pair_grad, other, preferred_element_type=f32)
    unit = unit.astype(f32)
    along = jnp.sum(unit * grad, -1, keepdims=True)
    return ((grad - unit * along) * (scale * LOGIT_SCALE)).T.astype(bf16)


def local(image_features, text_features, image_weight, text_weight, pair_index):
    zh = lax.axis_index("zh")
    img = lax.axis_index(IMG)
    txt = lax.axis_index(TXT)
    block_rows = image_features.shape[0]
    own_rows = block_rows // 16
    image_cols = image_features.shape[1]
    text_cols = text_features.shape[1]

    def by_own_rows(features, cols):
        padded = jnp.pad(features, ((0, 0), (0, LANES - cols)))
        return padded.reshape(16, own_rows, LANES).transpose(1, 0, 2).reshape(own_rows, 16 * LANES)

    def pick(one, two):
        return jnp.where(zh == 0, one, two)

    features = [by_own_rows(image_features, image_cols), by_own_rows(text_features, text_cols)]
    partials = exchange(head_partials(image_features, text_features, image_weight, text_weight), TXT)
    pairs = lax.dynamic_slice_in_dim(pair_index, txt * own_rows, own_rows, 0).astype(f32)[:, None]
    ids = (img * block_rows + txt * own_rows + jnp.arange(own_rows)).astype(f32)[:, None]
    first, second = unit_rows(partials, pairs, ids)

    n1_own, n1_given = pick(*first), pick(*first[::-1])
    n2_own, n2_given = pick(*second[::-1]), pick(*second)
    x_own, x_given = pick(*features), pick(*features[::-1])
    given = swap(jnp.concatenate([n1_given, x_given, n2_given], axis=1), "zh")
    width = n1_own.shape[1] + x_own.shape[1]
    n1_own = jnp.concatenate([n1_own, x_own], axis=1)
    n1_own = jnp.concatenate([pick(n1_own, given[:, :width]), pick(given[:, :width], n1_own)], axis=0)
    n2_own = jnp.concatenate([pick(n2_own, given[:, width:]), pick(given[:, width:], n2_own)], axis=0)

    column = exchange(jnp.tile(n2_own, (4, 1)), "zl")
    column, n1_own = lax.optimization_barrier((column, n1_own))
    block = [column] + [lax.ppermute(column, "x", [(i, i ^ step) for i in range(4)]) for step in (1, 2, 3)]
    block = jnp.concatenate(block, axis=0)
    n1 = exchange(jnp.tile(n1_own, (8, 1)), "y")
    terms = grad_terms(n1, [block, swap(block, "core")])

    chunk = E // 8
    dpre = jnp.sum(exchange(terms, "y").astype(f32).reshape(8, chunk, -1), axis=0).astype(bf16)
    dpre = exchange(jnp.tile(dpre, (16, 1)), TXT).reshape(16, chunk, -1)
    weight_grad = jnp.zeros((chunk, LANES), f32)
    for step in range(16):
        rows = n1[:, E + LANES * (step + 1) : E + LANES * (step + 2)]
        weight_grad = weight_grad + jnp.dot(dpre[step], rows, preferred_element_type=f32)
    both = lax.all_gather(weight_grad, "core", axis=0, tiled=False)
    weight_grad = jnp.sum(both, axis=0).astype(bf16)
    whole = exchange(jnp.tile(weight_grad, (16, 1)), ZY).astype(f32)
    return whole[:E, :image_cols].T, whole[E:, :text_cols].T


def solution(mesh):
    fine = Mesh(mesh.devices.reshape(2, 8, 2, 4, 4), AXES)
    in_specs = (P(IMG, TXT), P(IMG, TXT), P(TXT, None), P(TXT, None), P(IMG))
    out_specs = (P(TXT, None), P(TXT, None))
    return jax.shard_map(local, mesh=fine, in_specs=in_specs, out_specs=out_specs, check_vma=False)
```

time: 187 us -> 159 us (0.85)
  blocking collectives: 83.6 us -> 64 us
  waiting for transfers between devices: 47.1 us -> 33.4 us
  starting transfers between devices: 34.4 us -> 46.8 us
  matrix products: 9.69 us -> 6.14 us
  other arithmetic: 5.82 us -> 2.45 us
    all_to_all x3, blocking collectives: 77.9 us -> 55.7 us  [exchange(): return lax.all_to_all(value, axis, 0, 0, tiled=True)]
    ppermute x1 -> x5, starting transfers between devices: 5.9 us -> 25 us  [the longest x2 15.4 us: swap(): return lax.ppermute(value, axis, [(0, 1), (1, 0)])]
    all_to_all x3, waiting for transfers between devices: 45.7 us -> 30.2 us  [exchange(): return lax.all_to_all(value, axis, 0, 0, tiled=True)]
    all_to_all x3, starting transfers between devices: 28.5 us -> 21.8 us  [exchange(): return lax.all_to_all(value, axis, 0, 0, tiled=True)]
    dot_general x20 -> x18, matrix products: 7.46 us -> 3.91 us  [the longest x16 2.47 us: local(): jnp.dot(dpre[step], rows, preferred_element_type=f32)]
    all_gather x1, blocking collectives: 5.69 us -> 8.25 us  [local(): both = lax.all_gather(weight_grad, 'core', axis=0, tiled=False)]
    concatenate x4 -> x3, other arithmetic: 2.25 us -> 0.03 us  [the longest x1 0.01 us: local(): jnp.concatenate([pick(n1_own, given[:, :width]), pick(given[:, :width], n...]
  transfers between devices with their start and end apart: 4 -> 8, of which waited for: 4 -> 5; matrix products, arithmetic and copies ran while one was open for 2% -> 1% of each run, Pallas kernels for 0% -> 0%
where the time goes in v3:
time: 159 us; the launch traced here: 158 us
  blocking collectives  64 us (40%)
  starting transfers between devices  46.8 us (29%)
  waiting for transfers between devices  33.4 us (21%)
  matrix products  6.14 us (4%)
  local copies, waits for them, and re-layouts  4.33 us (3%)
  other arithmetic  2.45 us (2%)
    all_to_all x3, blocking collectives, exchange(): return lax.all_to_all(value, axis, 0, 0, tiled=True)  55.7 us
    all_to_all x3, waiting for transfers between devices, exchange(): return lax.all_to_all(value, axis, 0, 0, tiled=True)  30.2 us
    all_to_all x3, starting transfers between devices, exchange(): return lax.all_to_all(value, axis, 0, 0, tiled=True)  21.8 us
    ppermute x2, starting transfers between devices, swap(): return lax.ppermute(value, axis, [(0, 1), (1, 0)])  15.4 us
    ppermute x3, starting transfers between devices, local(): lax.ppermute(column, 'x', [(i, i ^ step) for i in range(4)])  9.57 us
    all_gather x1, blocking collectives, local(): both = lax.all_gather(weight_grad, 'core', axis=0, tiled=False)  8.25 us
    ppermute x2, waiting for transfers between devices, swap(): return lax.ppermute(value, axis, [(0, 1), (1, 0)])  3.23 us
  transfers between devices with their start and end apart: 8, of which 5 were waited for; matrix products, arithmetic and copies ran while one was open for 1% of the time, Pallas kernels for 0%

profile of v3, /device:TPU:1, one launch (start us, length us, event | category | flops | bytes accessed | tf_op | source)
XLA Modules:
  0.0 158.2 jit_solution(16813881105696404571)
XLA Ops:
  0.6 1.2 convolution_convert_fusion
  1.9 1.0 convolution_convert_fusion.1
  2.9 0.9 maximum_bitcast_fusion
  3.8 10.4 %all-to-all-start = ((bf16[16,8,2304]{2,1,0:T(8,128)(2,1)}), bf16[16,8,2304]{2,1,0:T(8,128)(2,1)S(1)}, u32[]{:S(2)}, u32[]{:S(2)}) async-start(bf16[16,8,2304]{2,1,0:T(8,128)(2,1)} %maximum_bitcast_fusion), calls=%async_computation | async-start | bytes 1179648 | tf_op jit(solution)/shard_map/all_to_all | solution.py:21
  14.6 14.4 %all-to-all-done = bf16[16,8,2304]{2,1,0:T(8,128)(2,1)S(1)} async-done(((bf16[16,8,2304]{2,1,0:T(8,128)(2,1)}), bf16[16,8,2304]{2,1,0:T(8,128)(2,1)S(1)}, u32[]{:S(2)}, u32[]{:S(2)}) %all-to-all-start) | async-done | bytes 589856 | tf_op jit(solution)/shard_map/all_to_all | solution.py:21
  29.5 7.9 %collective-permute-start = (bf16[8,4608]{1,0:T(8,128)(2,1)S(1)}, bf16[8,4608]{1,0:T(8,128)(2,1)S(1)}, u32[]{:S(2)}, u32[]{:S(2)}) collective-permute-start(bf16[8,4608]{1,0:T(8,128)(2,1)S(1)} %pad_maximum_fusion.1), channel_id=1, source_target_pairs={{0,256},{256,0},{1,257},{257,1},{2,258},{258,2},{3,259},{259,3},{4... | collective-permute-start | bytes 221192 | tf_op jit(solution)/shard_map/ppermute | solution.py:25
  37.4 1.7 %collective-permute-done = bf16[8,4608]{1,0:T(8,128)(2,1)S(1)} collective-permute-done((bf16[8,4608]{1,0:T(8,128)(2,1)S(1)}, bf16[8,4608]{1,0:T(8,128)(2,1)S(1)}, u32[]{:S(2)}, u32[]{:S(2)}) %collective-permute-start) | collective-permute-done | bytes 73760 | tf_op jit(solution)/shard_map/ppermute | solution.py:25
  39.9 4.6 %all-to-all-start.1 = ((bf16[4,16,1280]{2,1,0:T(8,128)(2,1)}), bf16[4,16,1280]{2,1,0:T(8,128)(2,1)S(1)}, u32[]{:S(2)}, u32[]{:S(2)}) async-start(bf16[4,16,1280]{2,1,0:T(8,128)(2,1)} %tile.8), calls=%async_computation.1 | async-start | bytes 327680 | tf_op jit(solution)/shard_map/all_to_all | solution.py:21
  44.5 4.8 %all-to-all-done.1 = bf16[4,16,1280]{2,1,0:T(8,128)(2,1)S(1)} async-done(((bf16[4,16,1280]{2,1,0:T(8,128)(2,1)}), bf16[4,16,1280]{2,1,0:T(8,128)(2,1)S(1)}, u32[]{:S(2)}, u32[]{:S(2)}) %all-to-all-start.1) | async-done | bytes 163872 | tf_op jit(solution)/shard_map/all_to_all | solution.py:21
  49.4 2.2 %collective-permute-start.1 = (bf16[64,1280]{1,0:T(8,128)(2,1)S(1)}, bf16[64,1280]{1,0:T(8,128)(2,1)S(1)}, u32[]{:S(2)}, u32[]{:S(2)}) collective-permute-start(bf16[64,1280]{1,0:T(8,128)(2,1)S(1)} %bitcast.104), channel_id=1, source_target_pairs={{0,1},{1,0},{2,3},{3,2},{4,5},{5,4},{6,7},{7,6},{8,9},{9,8},{10,11... | collective-permute-start | bytes 491528 | tf_op jit(solution)/shard_map/ppermute | solution.py:121
  51.5 3.4 %collective-permute-start.2 = (bf16[64,1280]{1,0:T(8,128)(2,1)S(1)}, bf16[64,1280]{1,0:T(8,128)(2,1)S(1)}, u32[]{:S(2)}, u32[]{:S(2)}) collective-permute-start(bf16[64,1280]{1,0:T(8,128)(2,1)S(1)} %bitcast.105), channel_id=1, source_target_pairs={{0,2},{1,3},{2,0},{3,1},{4,6},{5,7},{6,4},{7,5},{8,10},{9,11},{10,... | collective-permute-start | bytes 491528 | tf_op jit(solution)/shard_map/ppermute | solution.py:121
  55.0 4.0 %collective-permute-start.3 = (bf16[64,1280]{1,0:T(8,128)(2,1)S(1)}, bf16[64,1280]{1,0:T(8,128)(2,1)S(1)}, u32[]{:S(2)}, u32[]{:S(2)}) collective-permute-start(bf16[64,1280]{1,0:T(8,128)(2,1)S(1)} %bitcast.106), channel_id=1, source_target_pairs={{0,3},{1,2},{2,1},{3,0},{4,7},{5,6},{6,5},{7,4},{8,11},{9,10},{10,... | collective-permute-start | bytes 491528 | tf_op jit(solution)/shard_map/ppermute | solution.py:121
  58.9 1.0 tile.9
  59.9 6.8 %all-to-all-start.2 = ((bf16[8,16,3328]{2,1,0:T(8,128)(2,1)}), bf16[8,16,3328]{2,1,0:T(8,128)(2,1)S(1)}, u32[]{:S(2)}, u32[]{:S(2)}) async-start(bf16[8,16,3328]{2,1,0:T(8,128)(2,1)} %tile.9), calls=%async_computation.2 | async-start | bytes 1703936 | tf_op jit(solution)/shard_map/all_to_all | solution.py:21
  66.8 7.5 %collective-permute-start.4 = (bf16[256,1280]{1,0:T(8,128)(2,1)S(1)}, bf16[256,1280]{1,0:T(8,128)(2,1)S(1)}, u32[]{:S(2)}, u32[]{:S(2)}) collective-permute-start(bf16[256,1280]{1,0:T(8,128)(2,1)S(1)} %constant_dynamic-update-slice_fusion), channel_id=1, source_target_pairs={{0,16},{16,0},{1,17},{17,1},{2,18},{18,2},{3,19},{19,3},{4,20},{20... | collective-permute-start | bytes 1966088 | tf_op jit(solution)/shard_map/ppermute | solution.py:25
  74.5 1.5 collective-permute-done.4
  76.2 11.0 %all-to-all-done.2 = bf16[8,16,3328]{2,1,0:T(8,128)(2,1)S(1)} async-done(((bf16[8,16,3328]{2,1,0:T(8,128)(2,1)}), bf16[8,16,3328]{2,1,0:T(8,128)(2,1)S(1)}, u32[]{:S(2)}, u32[]{:S(2)}) %all-to-all-start.2) | async-done | bytes 852000 | tf_op jit(solution)/shard_map/all_to_all | solution.py:21
  88.0 0.8 fusion.15
  89.3 12.1 %all_to_all.48 = bf16[8,144,128]{2,1,0:T(8,128)(2,1)S(1)} all-to-all(bf16[8,144,128]{2,1,0:T(8,128)(2,1)S(1)} %bitcast.103), channel_id=1, replica_groups=mesh['zh'=2,'y'=8,'core'=2,'zl'=4,'x'=4] {'y'}, dimensions={0} | all-to-all | bytes 589824 | tf_op jit(solution)/shard_map/all_to_all | solution.py:21
  101.4 16.3 %all_to_all.49 = bf16[16,144,128]{2,1,0:T(8,128)(2,1)S(1)} all-to-all(bf16[16,144,128]{2,1,0:T(8,128)(2,1)S(1)} %tile.10), channel_id=1, replica_groups=mesh['zh'=2,'y'=8,'core'=2,'zl'=4,'x'=4] {'zl','x'}, dimensions={0} | all-to-all | bytes 1179648 | tf_op jit(solution)/shard_map/all_to_all | solution.py:21
  120.3 8.2 %all-gather = f32[288,128]{1,0:T(8,128)S(1)} all-gather(f32[144,128]{1,0:T(8,128)S(1)} %convolution_add_fusion.1), channel_id=2, replica_groups=mesh['zh'=2,'y'=8,'core'=2,'zl'=4,'x'=4] {'core'}, dimensions={0}, use_global_device_ids=true | all-gather | bytes 221184 | tf_op jit(solution)/shard_map/all_gather | solution.py:133
  128.6 27.4 %all_to_all.50 = bf16[16,144,128]{2,1,0:T(8,128)(2,1)S(1)} all-to-all(bf16[16,144,128]{2,1,0:T(8,128)(2,1)S(1)} %tile.11), channel_id=1, replica_groups=mesh['zh'=2,'y'=8,'core'=2,'zl'=4,'x'=4] {'zh','y'}, dimensions={0} | all-to-all | bytes 1179648 | tf_op jit(solution)/shard_map/all_to_all | solution.py:21
  156.3 1.0 copy.16
  157.2 0.9 copy.17
  (67 shorter events, 6.2 us)
Async XLA Ops:
  0.6 1.3 copy-start
  2.9 11.3 %copy-start.1 = (bf16[128,96]{0,1:T(8,128)(2,1)S(1)}, bf16[128,96]{0,1:T(8,128)(2,1)}, u32[]{:S(2)}) copy-start(bf16[128,96]{0,1:T(8,128)(2,1)} %param.5) | copy-start | bytes 73732
  2.9 11.4 %copy-start.2 = (bf16[128,72]{0,1:T(8,128)(2,1)S(1)}, bf16[128,72]{0,1:T(8,128)(2,1)}, u32[]{:S(2)}) copy-start(bf16[128,72]{0,1:T(8,128)(2,1)} %param.6) | copy-start | bytes 55300
  2.9 11.6 %copy-start.3 = (s32[128]{0:T(128)S(1)}, s32[128]{0:T(128)}, u32[]{:S(2)}) copy-start(s32[128]{0:T(128)} %param.9) | copy-start | bytes 1540
  3.8 25.2 %all-to-all-start = ((bf16[16,8,2304]{2,1,0:T(8,128)(2,1)}), bf16[16,8,2304]{2,1,0:T(8,128)(2,1)S(1)}, u32[]{:S(2)}, u32[]{:S(2)}) async-start(bf16[16,8,2304]{2,1,0:T(8,128)(2,1)} %maximum_bitcast_fusion), calls=%async_computation | async-start | bytes 1179648 | tf_op jit(solution)/shard_map/all_to_all | solution.py:21
  29.5 9.7 %collective-permute-start = (bf16[8,4608]{1,0:T(8,128)(2,1)S(1)}, bf16[8,4608]{1,0:T(8,128)(2,1)S(1)}, u32[]{:S(2)}, u32[]{:S(2)}) collective-permute-start(bf16[8,4608]{1,0:T(8,128)(2,1)S(1)} %pad_maximum_fusion.1), channel_id=1, source_target_pairs={{0,256},{256,0},{1,257},{257,1},{2,258},{258,2},{3,259},{259,3},{4... | collective-permute-start | bytes 221192 | tf_op jit(solution)/shard_map/ppermute | solution.py:25
  39.9 9.5 %all-to-all-start.1 = ((bf16[4,16,1280]{2,1,0:T(8,128)(2,1)}), bf16[4,16,1280]{2,1,0:T(8,128)(2,1)S(1)}, u32[]{:S(2)}, u32[]{:S(2)}) async-start(bf16[4,16,1280]{2,1,0:T(8,128)(2,1)} %tile.8), calls=%async_computation.1 | async-start | bytes 327680 | tf_op jit(solution)/shard_map/all_to_all | solution.py:21
  49.4 17.4 %collective-permute-start.1 = (bf16[64,1280]{1,0:T(8,128)(2,1)S(1)}, bf16[64,1280]{1,0:T(8,128)(2,1)S(1)}, u32[]{:S(2)}, u32[]{:S(2)}) collective-permute-start(bf16[64,1280]{1,0:T(8,128)(2,1)S(1)} %bitcast.104), channel_id=1, source_target_pairs={{0,1},{1,0},{2,3},{3,2},{4,5},{5,4},{6,7},{7,6},{8,9},{9,8},{10,11... | collective-permute-start | bytes 491528 | tf_op jit(solution)/shard_map/ppermute | solution.py:121
  51.5 15.2 %collective-permute-start.2 = (bf16[64,1280]{1,0:T(8,128)(2,1)S(1)}, bf16[64,1280]{1,0:T(8,128)(2,1)S(1)}, u32[]{:S(2)}, u32[]{:S(2)}) collective-permute-start(bf16[64,1280]{1,0:T(8,128)(2,1)S(1)} %bitcast.105), channel_id=1, source_target_pairs={{0,2},{1,3},{2,0},{3,1},{4,6},{5,7},{6,4},{7,5},{8,10},{9,11},{10,... | collective-permute-start | bytes 491528 | tf_op jit(solution)/shard_map/ppermute | solution.py:121
  55.0 11.9 %collective-permute-start.3 = (bf16[64,1280]{1,0:T(8,128)(2,1)S(1)}, bf16[64,1280]{1,0:T(8,128)(2,1)S(1)}, u32[]{:S(2)}, u32[]{:S(2)}) collective-permute-start(bf16[64,1280]{1,0:T(8,128)(2,1)S(1)} %bitcast.106), channel_id=1, source_target_pairs={{0,3},{1,2},{2,1},{3,0},{4,7},{5,6},{6,5},{7,4},{8,11},{9,10},{10,... | collective-permute-start | bytes 491528 | tf_op jit(solution)/shard_map/ppermute | solution.py:121
  59.9 27.2 %all-to-all-start.2 = ((bf16[8,16,3328]{2,1,0:T(8,128)(2,1)}), bf16[8,16,3328]{2,1,0:T(8,128)(2,1)S(1)}, u32[]{:S(2)}, u32[]{:S(2)}) async-start(bf16[8,16,3328]{2,1,0:T(8,128)(2,1)} %tile.9), calls=%async_computation.2 | async-start | bytes 1703936 | tf_op jit(solution)/shard_map/all_to_all | solution.py:21
  66.8 9.2 %collective-permute-start.4 = (bf16[256,1280]{1,0:T(8,128)(2,1)S(1)}, bf16[256,1280]{1,0:T(8,128)(2,1)S(1)}, u32[]{:S(2)}, u32[]{:S(2)}) collective-permute-start(bf16[256,1280]{1,0:T(8,128)(2,1)S(1)} %constant_dynamic-update-slice_fusion), channel_id=1, source_target_pairs={{0,16},{16,0},{1,17},{17,1},{2,18},{18,2},{3,19},{19,3},{4,20},{20... | collective-permute-start | bytes 1966088 | tf_op jit(solution)/shard_map/ppermute | solution.py:25

commit v4 on v3

--- a/solution.py
+++ b/solution.py
@@ -108,19 +108,17 @@
     first, second = unit_rows(partials, pairs, ids)
 
     n1_own, n1_given = pick(*first), pick(*first[::-1])
-    n2_own, n2_given = pick(*second[::-1]), pick(*second)
     x_own, x_given = pick(*features), pick(*features[::-1])
-    given = swap(jnp.concatenate([n1_given, x_given, n2_given], axis=1), "zh")
-    width = n1_own.shape[1] + x_own.shape[1]
     n1_own = jnp.concatenate([n1_own, x_own], axis=1)
-    n1_own = jnp.concatenate([pick(n1_own, given[:, :width]), pick(given[:, :width], n1_own)], axis=0)
-    n2_own = jnp.concatenate([pick(n2_own, given[:, width:]), pick(given[:, width:], n2_own)], axis=0)
+    given = swap(jnp.concatenate([n1_given, x_given], axis=1), "zh")
+    n1_own = jnp.concatenate([pick(n1_own, given), pick(given, n1_own)], axis=0)
 
-    column = exchange(jnp.tile(n2_own, (4, 1)), "zl")
+    column = exchange(jnp.concatenate([jnp.tile(second[1], (4, 1)), jnp.tile(second[0], (4, 1))], axis=0), ("zh", "zl"))
     column, n1_own = lax.optimization_barrier((column, n1_own))
     block = [column] + [lax.ppermute(column, "x", [(i, i ^ step) for i in range(4)]) for step in (1, 2, 3)]
     block = jnp.concatenate(block, axis=0)
     n1 = exchange(jnp.tile(n1_own, (8, 1)), "y")
+    block, n1 = lax.optimization_barrier((block, n1))
     terms = grad_terms(n1, [block, swap(block, "core")])
 
     chunk = E // 8
@@ -131,8 +129,11 @@
         rows = n1[:, E + LANES * (step + 1) : E + LANES * (step + 2)]
         weight_grad = weight_grad + jnp.dot(dpre[step], rows, preferred_element_type=f32)
     both = lax.all_gather(weight_grad, "core", axis=0, tiled=False)
-    weight_grad = jnp.sum(both, axis=0).astype(bf16)
-    whole = exchange(jnp.tile(weight_grad, (16, 1)), ZY).astype(f32)
+    half = chunk // 2
+    weight_grad = lax.dynamic_slice_in_dim(jnp.sum(both, axis=0), lax.axis_index("core") * half, half, 0).astype(bf16)
+    halves = exchange(jnp.tile(weight_grad, (16, 1)), ZY)
+    whole = lax.all_gather(halves, "core", axis=0, tiled=False).reshape(2, 16, half, LANES).astype(f32)
+    whole = whole.transpose(1, 0, 2, 3).reshape(2 * E, LANES)
     return whole[:E, :image_cols].T, whole[E:, :text_cols].T
 
 

time: 159 us -> 154 us (0.969)
  blocking collectives: 64 us -> 39.2 us
  waiting for transfers between devices: 33.4 us -> 50.5 us
    all_to_all x3 -> x2, blocking collectives: 55.7 us -> 31.1 us  [exchange(): return lax.all_to_all(value, axis, 0, 0, tiled=True)]
    all_to_all x3 -> x4, waiting for transfers between devices: 30.2 us -> 44.5 us  [exchange(): return lax.all_to_all(value, axis, 0, 0, tiled=True)]
    ppermute x3, waiting for transfers between devices: 0.01 us -> 5.38 us  [local(): lax.ppermute(column, 'x', [(i, i ^ step) for i in range(4)])]
    all_gather x1, blocking collectives: 8.25 us -> 4.17 us  [local(): both = lax.all_gather(weight_grad, 'core', axis=0, tiled=False)]
    all_gather x0 -> x1, blocking collectives: none -> 3.91 us  [local(): lax.all_gather(halves, 'core', axis=0, tiled=False)]
    all_to_all x3 -> x4, starting transfers between devices: 21.8 us -> 25.4 us  [exchange(): return lax.all_to_all(value, axis, 0, 0, tiled=True)]
    ppermute x2, waiting for transfers between devices: 3.23 us -> 0.6 us  [swap(): return lax.ppermute(value, axis, [(0, 1), (1, 0)])]
    ppermute x2, starting transfers between devices: 15.4 us -> 13.3 us  [swap(): return lax.ppermute(value, axis, [(0, 1), (1, 0)])]
  transfers between devices with their start and end apart: 8 -> 9, of which waited for: 5 -> 7; matrix products, arithmetic and copies ran while one was open for 1% -> 1% of each run, Pallas kernels for 0% -> 0%
where the time goes in v4:
time: 154 us; the launch traced here: 153 us
  waiting for transfers between devices  50.5 us (33%)
  starting transfers between devices  48.3 us (31%)
  blocking collectives  39.2 us (25%)
  matrix products  6.15 us (4%)
  local copies, waits for them, and re-layouts  4.49 us (3%)
  other arithmetic  3.11 us (2%)
    all_to_all x4, waiting for transfers between devices, exchange(): return lax.all_to_all(value, axis, 0, 0, tiled=True)  44.5 us
    all_to_all x2, blocking collectives, exchange(): return lax.all_to_all(value, axis, 0, 0, tiled=True)  31.1 us
    all_to_all x4, starting transfers between devices, exchange(): return lax.all_to_all(value, axis, 0, 0, tiled=True)  25.4 us
    ppermute x2, starting transfers between devices, swap(): return lax.ppermute(value, axis, [(0, 1), (1, 0)])  13.3 us
    ppermute x3, starting transfers between devices, local(): lax.ppermute(column, 'x', [(i, i ^ step) for i in range(4)])  9.57 us
    ppermute x3, waiting for transfers between devices, local(): lax.ppermute(column, 'x', [(i, i ^ step) for i in range(4)])  5.38 us
    all_gather x1, blocking collectives, local(): both = lax.all_gather(weight_grad, 'core', axis=0, tiled=False)  4.17 us
    all_gather x1, blocking collectives, local(): lax.all_gather(halves, 'core', axis=0, tiled=False)  3.91 us
  transfers between devices with their start and end apart: 9, of which 7 were waited for; matrix products, arithmetic and copies ran while one was open for 1% of the time, Pallas kernels for 0%

profile of v4, /device:TPU:1, one launch (start us, length us, event | category | flops | bytes accessed | tf_op | source)
XLA Modules:
  0.0 152.9 jit_solution(11259939438980408997)
XLA Ops:
  0.6 1.2 convolution_convert_fusion
  1.9 1.0 convolution_convert_fusion.1
  3.8 10.4 %all-to-all-start = ((bf16[16,8,2304]{2,1,0:T(8,128)(2,1)}), bf16[16,8,2304]{2,1,0:T(8,128)(2,1)S(1)}, u32[]{:S(2)}, u32[]{:S(2)}) async-start(bf16[16,8,2304]{2,1,0:T(8,128)(2,1)} %maximum_bitcast_fusion), calls=%async_computation | async-start | bytes 1179648 | tf_op jit(solution)/shard_map/all_to_all | solution.py:21
  14.6 14.4 %all-to-all-done = bf16[16,8,2304]{2,1,0:T(8,128)(2,1)S(1)} async-done(((bf16[16,8,2304]{2,1,0:T(8,128)(2,1)}), bf16[16,8,2304]{2,1,0:T(8,128)(2,1)S(1)}, u32[]{:S(2)}, u32[]{:S(2)}) %all-to-all-start) | async-done | bytes 589856 | tf_op jit(solution)/shard_map/all_to_all | solution.py:21
  29.5 7.9 %collective-permute-start = (bf16[8,3328]{1,0:T(8,128)(2,1)S(1)}, bf16[8,3328]{1,0:T(8,128)(2,1)S(1)}, u32[]{:S(2)}, u32[]{:S(2)}) collective-permute-start(bf16[8,3328]{1,0:T(8,128)(2,1)S(1)} %pad_maximum_fusion.3), channel_id=1, source_target_pairs={{0,256},{256,0},{1,257},{257,1},{2,258},{258,2},{3,259},{259,3},{4... | collective-permute-start | bytes 159752 | tf_op jit(solution)/shard_map/ppermute | solution.py:25
  38.1 4.6 %all-to-all-start.1 = ((bf16[8,8,1280]{2,1,0:T(8,128)(2,1)}), bf16[8,8,1280]{2,1,0:T(8,128)(2,1)S(1)}, u32[]{:S(2)}, u32[]{:S(2)}) async-start(bf16[8,8,1280]{2,1,0:T(8,128)(2,1)} %maximum_bitcast_fusion.1), calls=%async_computation.1 | async-start | bytes 327680 | tf_op jit(solution)/shard_map/all_to_all | solution.py:21
  42.8 8.3 %all-to-all-done.1 = bf16[8,8,1280]{2,1,0:T(8,128)(2,1)S(1)} async-done(((bf16[8,8,1280]{2,1,0:T(8,128)(2,1)}), bf16[8,8,1280]{2,1,0:T(8,128)(2,1)S(1)}, u32[]{:S(2)}, u32[]{:S(2)}) %all-to-all-start.1) | async-done | bytes 163872 | tf_op jit(solution)/shard_map/all_to_all | solution.py:21
  51.1 1.0 tile.18
  52.1 6.8 %all-to-all-start.2 = ((bf16[8,16,3328]{2,1,0:T(8,128)(2,1)}), bf16[8,16,3328]{2,1,0:T(8,128)(2,1)S(1)}, u32[]{:S(2)}, u32[]{:S(2)}) async-start(bf16[8,16,3328]{2,1,0:T(8,128)(2,1)} %tile.18), calls=%async_computation.2 | async-start | bytes 1703936 | tf_op jit(solution)/shard_map/all_to_all | solution.py:21
  58.9 2.2 %collective-permute-start.1 = (bf16[64,1280]{1,0:T(8,128)(2,1)S(1)}, bf16[64,1280]{1,0:T(8,128)(2,1)S(1)}, u32[]{:S(2)}, u32[]{:S(2)}) collective-permute-start(bf16[64,1280]{1,0:T(8,128)(2,1)S(1)} %bitcast.117), channel_id=1, source_target_pairs={{0,1},{1,0},{2,3},{3,2},{4,5},{5,4},{6,7},{7,6},{8,9},{9,8},{10,11... | collective-permute-start | bytes 491528 | tf_op jit(solution)/shard_map/ppermute | solution.py:118
  61.1 3.5 %collective-permute-start.2 = (bf16[64,1280]{1,0:T(8,128)(2,1)S(1)}, bf16[64,1280]{1,0:T(8,128)(2,1)S(1)}, u32[]{:S(2)}, u32[]{:S(2)}) collective-permute-start(bf16[64,1280]{1,0:T(8,128)(2,1)S(1)} %bitcast.118), channel_id=1, source_target_pairs={{0,2},{1,3},{2,0},{3,1},{4,6},{5,7},{6,4},{7,5},{8,10},{9,11},{10,... | collective-permute-start | bytes 491528 | tf_op jit(solution)/shard_map/ppermute | solution.py:118
  64.5 3.9 %collective-permute-start.3 = (bf16[64,1280]{1,0:T(8,128)(2,1)S(1)}, bf16[64,1280]{1,0:T(8,128)(2,1)S(1)}, u32[]{:S(2)}, u32[]{:S(2)}) collective-permute-start(bf16[64,1280]{1,0:T(8,128)(2,1)S(1)} %bitcast.119), channel_id=1, source_target_pairs={{0,3},{1,2},{2,1},{3,0},{4,7},{5,6},{6,5},{7,4},{8,11},{9,10},{10,... | collective-permute-start | bytes 491528 | tf_op jit(solution)/shard_map/ppermute | solution.py:118
  68.5 1.3 collective-permute-done.2
  69.8 4.1 %collective-permute-done.3 = bf16[64,1280]{1,0:T(8,128)(2,1)S(1)} collective-permute-done((bf16[64,1280]{1,0:T(8,128)(2,1)S(1)}, bf16[64,1280]{1,0:T(8,128)(2,1)S(1)}, u32[]{:S(2)}, u32[]{:S(2)}) %collective-permute-start.3) | collective-permute-done | bytes 163872 | tf_op jit(solution)/shard_map/ppermute | solution.py:118
  73.9 7.0 %all-to-all-done.2 = bf16[8,16,3328]{2,1,0:T(8,128)(2,1)S(1)} async-done(((bf16[8,16,3328]{2,1,0:T(8,128)(2,1)}), bf16[8,16,3328]{2,1,0:T(8,128)(2,1)S(1)}, u32[]{:S(2)}, u32[]{:S(2)}) %all-to-all-start.2) | async-done | bytes 852000 | tf_op jit(solution)/shard_map/all_to_all | solution.py:21
  80.9 5.4 %collective-permute-start.4 = (bf16[256,1280]{1,0:T(8,128)(2,1)S(1)}, bf16[256,1280]{1,0:T(8,128)(2,1)S(1)}, u32[]{:S(2)}, u32[]{:S(2)}) collective-permute-start(bf16[256,1280]{1,0:T(8,128)(2,1)S(1)} %pad_maximum_fusion), channel_id=1, source_target_pairs={{0,16},{16,0},{1,17},{17,1},{2,18},{18,2},{3,19},{19,3},{4,20},{20... | collective-permute-start | bytes 1966088 | tf_op jit(solution)/shard_map/ppermute | solution.py:25
  89.4 15.0 %all_to_all.51 = bf16[8,144,128]{2,1,0:T(8,128)(2,1)S(1)} all-to-all(bf16[8,144,128]{2,1,0:T(8,128)(2,1)S(1)} %bitcast.116), channel_id=1, replica_groups=mesh['zh'=2,'y'=8,'core'=2,'zl'=4,'x'=4] {'y'}, dimensions={0} | all-to-all | bytes 589824 | tf_op jit(solution)/shard_map/all_to_all | solution.py:21
  105.4 3.6 %all-to-all-start.4 = ((bf16[16,144,128]{2,1,0:T(8,128)(2,1)}), bf16[16,144,128]{2,1,0:T(8,128)(2,1)S(1)}, u32[]{:S(2)}, u32[]{:S(2)}) async-start(bf16[16,144,128]{2,1,0:T(8,128)(2,1)} %tile.19), calls=%async_computation.4 | async-start | bytes 1179648 | tf_op jit(solution)/shard_map/all_to_all | solution.py:21
  109.0 14.9 %all-to-all-done.4 = bf16[16,144,128]{2,1,0:T(8,128)(2,1)S(1)} async-done(((bf16[16,144,128]{2,1,0:T(8,128)(2,1)}), bf16[16,144,128]{2,1,0:T(8,128)(2,1)S(1)}, u32[]{:S(2)}, u32[]{:S(2)}) %all-to-all-start.4) | async-done | bytes 589856 | tf_op jit(solution)/shard_map/all_to_all | solution.py:21
  126.4 4.2 %all-gather = f32[288,128]{1,0:T(8,128)S(1)} all-gather(f32[144,128]{1,0:T(8,128)S(1)} %convolution_add_fusion.1), channel_id=2, replica_groups=mesh['zh'=2,'y'=8,'core'=2,'zl'=4,'x'=4] {'core'}, dimensions={0}, use_global_device_ids=true | all-gather | bytes 221184 | tf_op jit(solution)/shard_map/all_gather | solution.py:131
  130.7 16.1 %all_to_all.52 = bf16[16,72,128]{2,1,0:T(8,128)(2,1)S(1)} all-to-all(bf16[16,72,128]{2,1,0:T(8,128)(2,1)S(1)} %tile.20), channel_id=1, replica_groups=mesh['zh'=2,'y'=8,'core'=2,'zl'=4,'x'=4] {'zh','y'}, dimensions={0} | all-to-all | bytes 589824 | tf_op jit(solution)/shard_map/all_to_all | solution.py:21
  146.8 3.9 %all_gather.15 = bf16[2,1152,128]{2,1,0:T(8,128)(2,1)S(1)} all-gather(bf16[1,1152,128]{2,1,0:T(8,128)(2,1)S(1)} %bitcast.115), channel_id=1, replica_groups=mesh['zh'=2,'y'=8,'core'=2,'zl'=4,'x'=4] {'core'}, dimensions={0}, use_global_device_ids=true | all-gather | bytes 884736 | tf_op jit(solution)/shard_map/all_gather | solution.py:135
  150.9 1.0 copy.25
  151.9 0.9 copy.26
  (68 shorter events, 9.2 us)
Async XLA Ops:
  0.6 1.3 copy-start
  2.9 11.3 %copy-start.1 = (bf16[128,96]{0,1:T(8,128)(2,1)S(1)}, bf16[128,96]{0,1:T(8,128)(2,1)}, u32[]{:S(2)}) copy-start(bf16[128,96]{0,1:T(8,128)(2,1)} %param.5) | copy-start | bytes 73732
  2.9 11.4 %copy-start.2 = (bf16[128,72]{0,1:T(8,128)(2,1)S(1)}, bf16[128,72]{0,1:T(8,128)(2,1)}, u32[]{:S(2)}) copy-start(bf16[128,72]{0,1:T(8,128)(2,1)} %param.6) | copy-start | bytes 55300
  2.9 11.6 %copy-start.3 = (s32[128]{0:T(128)S(1)}, s32[128]{0:T(128)}, u32[]{:S(2)}) copy-start(s32[128]{0:T(128)} %param.9) | copy-start | bytes 1540
  3.8 25.2 %all-to-all-start = ((bf16[16,8,2304]{2,1,0:T(8,128)(2,1)}), bf16[16,8,2304]{2,1,0:T(8,128)(2,1)S(1)}, u32[]{:S(2)}, u32[]{:S(2)}) async-start(bf16[16,8,2304]{2,1,0:T(8,128)(2,1)} %maximum_bitcast_fusion), calls=%async_computation | async-start | bytes 1179648 | tf_op jit(solution)/shard_map/all_to_all | solution.py:21
  29.5 13.3 %collective-permute-start = (bf16[8,3328]{1,0:T(8,128)(2,1)S(1)}, bf16[8,3328]{1,0:T(8,128)(2,1)S(1)}, u32[]{:S(2)}, u32[]{:S(2)}) collective-permute-start(bf16[8,3328]{1,0:T(8,128)(2,1)S(1)} %pad_maximum_fusion.3), channel_id=1, source_target_pairs={{0,256},{256,0},{1,257},{257,1},{2,258},{258,2},{3,259},{259,3},{4... | collective-permute-start | bytes 159752 | tf_op jit(solution)/shard_map/ppermute | solution.py:25
  38.1 13.0 %all-to-all-start.1 = ((bf16[8,8,1280]{2,1,0:T(8,128)(2,1)}), bf16[8,8,1280]{2,1,0:T(8,128)(2,1)S(1)}, u32[]{:S(2)}, u32[]{:S(2)}) async-start(bf16[8,8,1280]{2,1,0:T(8,128)(2,1)} %maximum_bitcast_fusion.1), calls=%async_computation.1 | async-start | bytes 327680 | tf_op jit(solution)/shard_map/all_to_all | solution.py:21
  52.1 28.8 %all-to-all-start.2 = ((bf16[8,16,3328]{2,1,0:T(8,128)(2,1)}), bf16[8,16,3328]{2,1,0:T(8,128)(2,1)S(1)}, u32[]{:S(2)}, u32[]{:S(2)}) async-start(bf16[8,16,3328]{2,1,0:T(8,128)(2,1)} %tile.18), calls=%async_computation.2 | async-start | bytes 1703936 | tf_op jit(solution)/shard_map/all_to_all | solution.py:21
  58.9 9.6 %collective-permute-start.1 = (bf16[64,1280]{1,0:T(8,128)(2,1)S(1)}, bf16[64,1280]{1,0:T(8,128)(2,1)S(1)}, u32[]{:S(2)}, u32[]{:S(2)}) collective-permute-start(bf16[64,1280]{1,0:T(8,128)(2,1)S(1)} %bitcast.117), channel_id=1, source_target_pairs={{0,1},{1,0},{2,3},{3,2},{4,5},{5,4},{6,7},{7,6},{8,9},{9,8},{10,11... | collective-permute-start | bytes 491528 | tf_op jit(solution)/shard_map/ppermute | solution.py:118
  61.1 8.7 %collective-permute-start.2 = (bf16[64,1280]{1,0:T(8,128)(2,1)S(1)}, bf16[64,1280]{1,0:T(8,128)(2,1)S(1)}, u32[]{:S(2)}, u32[]{:S(2)}) collective-permute-start(bf16[64,1280]{1,0:T(8,128)(2,1)S(1)} %bitcast.118), channel_id=1, source_target_pairs={{0,2},{1,3},{2,0},{3,1},{4,6},{5,7},{6,4},{7,5},{8,10},{9,11},{10,... | collective-permute-start | bytes 491528 | tf_op jit(solution)/shard_map/ppermute | solution.py:118
  64.5 9.3 %collective-permute-start.3 = (bf16[64,1280]{1,0:T(8,128)(2,1)S(1)}, bf16[64,1280]{1,0:T(8,128)(2,1)S(1)}, u32[]{:S(2)}, u32[]{:S(2)}) collective-permute-start(bf16[64,1280]{1,0:T(8,128)(2,1)S(1)} %bitcast.119), channel_id=1, source_target_pairs={{0,3},{1,2},{2,1},{3,0},{4,7},{5,6},{6,5},{7,4},{8,11},{9,10},{10,... | collective-permute-start | bytes 491528 | tf_op jit(solution)/shard_map/ppermute | solution.py:118
  80.9 7.1 %collective-permute-start.4 = (bf16[256,1280]{1,0:T(8,128)(2,1)S(1)}, bf16[256,1280]{1,0:T(8,128)(2,1)S(1)}, u32[]{:S(2)}, u32[]{:S(2)}) collective-permute-start(bf16[256,1280]{1,0:T(8,128)(2,1)S(1)} %pad_maximum_fusion), channel_id=1, source_target_pairs={{0,16},{16,0},{1,17},{17,1},{2,18},{18,2},{3,19},{19,3},{4,20},{20... | collective-permute-start | bytes 1966088 | tf_op jit(solution)/shard_map/ppermute | solution.py:25
  105.4 18.5 %all-to-all-start.4 = ((bf16[16,144,128]{2,1,0:T(8,128)(2,1)}), bf16[16,144,128]{2,1,0:T(8,128)(2,1)S(1)}, u32[]{:S(2)}, u32[]{:S(2)}) async-start(bf16[16,144,128]{2,1,0:T(8,128)(2,1)} %tile.19), calls=%async_computation.4 | async-start | bytes 1179648 | tf_op jit(solution)/shard_map/all_to_all | solution.py:21

commit v5 on v4

--- a/solution.py
+++ b/solution.py
@@ -1,6 +1,7 @@
 import jax
 import jax.numpy as jnp
 from jax import lax
+from jax.experimental import pallas as pl
 from jax.sharding import Mesh
 from jax.sharding import PartitionSpec as P
 
@@ -25,10 +26,27 @@
     return lax.ppermute(value, axis, [(0, 1), (1, 0)])
 
 
+def head_kernel(image_ref, text_ref, image_weight_ref, text_weight_ref, out_ref):
+    tn = (((0,), (0,)), ((), ()))
+    for tower, (features, weight) in enumerate(((image_ref, image_weight_ref), (text_ref, text_weight_ref))):
+        rows = features[...]
+        out_ref[:, tower * E : (tower + 1) * E] = lax.dot_general(
+            rows, weight[...], tn, preferred_element_type=f32
+        ).astype(bf16)
+        square = (rows.shape[0], LANES)
+        same = lax.broadcasted_iota(jnp.int32, square, 0) == lax.broadcasted_iota(jnp.int32, square, 1)
+        place = jnp.where(same, 1.0, 0.0).astype(bf16)
+        out_ref[:, 2 * E + tower * LANES : 2 * E + (tower + 1) * LANES] = lax.dot_general(
+            rows, place, tn, preferred_element_type=f32
+        ).astype(bf16)
+
+
 def head_partials(image_features, text_features, image_weight, text_weight):
-    image = jnp.dot(image_features, image_weight, preferred_element_type=f32)
-    text = jnp.dot(text_features, text_weight, preferred_element_type=f32)
-    return jnp.concatenate([image.astype(bf16), text.astype(bf16)], axis=1)
+    return pl.pallas_call(
+        head_kernel,
+        out_shape=jax.ShapeDtypeStruct((image_features.shape[0], 2 * E + 2 * LANES), bf16),
+        name="head_partials",
+    )(image_features.T, text_features.T, image_weight, text_weight)
 
 
 def columns_in_lanes(columns, rows):
@@ -51,7 +69,7 @@
 
 def unit_rows(partials, pairs, ids):
     rows = partials.shape[0] // 16
-    total = jnp.sum(partials.astype(f32).reshape(16, rows, 2 * E), axis=0)
+    total = jnp.sum(partials[:, : 2 * E].astype(f32).reshape(16, rows, 2 * E), axis=0)
     first, second = [], []
     for tower, (key1, key2) in enumerate(((pairs, pairs), (ids, ids))):
         pre = total[:, tower * E : (tower + 1) * E]
@@ -94,15 +112,16 @@
     image_cols = image_features.shape[1]
     text_cols = text_features.shape[1]
 
-    def by_own_rows(features, cols):
-        padded = jnp.pad(features, ((0, 0), (0, LANES - cols)))
-        return padded.reshape(16, own_rows, LANES).transpose(1, 0, 2).reshape(own_rows, 16 * LANES)
-
     def pick(one, two):
         return jnp.where(zh == 0, one, two)
 
-    features = [by_own_rows(image_features, image_cols), by_own_rows(text_features, text_cols)]
     partials = exchange(head_partials(image_features, text_features, image_weight, text_weight), TXT)
+
+    def all_features(tower):
+        part = partials[:, 2 * E + tower * LANES : 2 * E + (tower + 1) * LANES]
+        return part.reshape(16, own_rows, LANES).transpose(1, 0, 2).reshape(own_rows, 16 * LANES)
+
+    features = [all_features(0), all_features(1)]
     pairs = lax.dynamic_slice_in_dim(pair_index, txt * own_rows, own_rows, 0).astype(f32)[:, None]
     ids = (img * block_rows + txt * own_rows + jnp.arange(own_rows)).astype(f32)[:, None]
     first, second = unit_rows(partials, pairs, ids)
@@ -114,23 +133,26 @@
     n1_own = jnp.concatenate([pick(n1_own, given), pick(given, n1_own)], axis=0)
 
     column = exchange(jnp.concatenate([jnp.tile(second[1], (4, 1)), jnp.tile(second[0], (4, 1))], axis=0), ("zh", "zl"))
-    column, n1_own = lax.optimization_barrier((column, n1_own))
     block = [column] + [lax.ppermute(column, "x", [(i, i ^ step) for i in range(4)]) for step in (1, 2, 3)]
     block = jnp.concatenate(block, axis=0)
     n1 = exchange(jnp.tile(n1_own, (8, 1)), "y")
-    block, n1 = lax.optimization_barrier((block, n1))
     terms = grad_terms(n1, [block, swap(block, "core")])
 
+    features = n1[:, E + LANES :]
+    terms, features = lax.optimization_barrier((terms, features))
+    other_features = swap(features, "core")
     chunk = E // 8
-    dpre = jnp.sum(exchange(terms, "y").astype(f32).reshape(8, chunk, -1), axis=0).astype(bf16)
-    dpre = exchange(jnp.tile(dpre, (16, 1)), TXT).reshape(16, chunk, -1)
-    weight_grad = jnp.zeros((chunk, LANES), f32)
-    for step in range(16):
-        rows = n1[:, E + LANES * (step + 1) : E + LANES * (step + 2)]
-        weight_grad = weight_grad + jnp.dot(dpre[step], rows, preferred_element_type=f32)
-    both = lax.all_gather(weight_grad, "core", axis=0, tiled=False)
     half = chunk // 2
-    weight_grad = lax.dynamic_slice_in_dim(jnp.sum(both, axis=0), lax.axis_index("core") * half, half, 0).astype(bf16)
+    core = lax.axis_index("core")
+    parts, other_features = lax.optimization_barrier((exchange(terms, "y"), other_features))
+    dpre = jnp.sum(parts.astype(f32).reshape(8, chunk, -1), axis=0).astype(bf16)
+    kept = jnp.where(core == 0, dpre[:half], dpre[half:])
+    given = swap(jnp.where(core == 0, dpre[half:], dpre[:half]), "core")
+    weight_grad = jnp.dot(kept, features, preferred_element_type=f32)
+    weight_grad = weight_grad + jnp.dot(given, other_features, preferred_element_type=f32)
+    parts = weight_grad.astype(bf16).reshape(half, 16, LANES).transpose(1, 0, 2).reshape(16 * half, LANES)
+    parts = exchange(parts, TXT).astype(f32).reshape(16, half, LANES)
+    weight_grad = jnp.sum(parts, axis=0).astype(bf16)
     halves = exchange(jnp.tile(weight_grad, (16, 1)), ZY)
     whole = lax.all_gather(halves, "core", axis=0, tiled=False).reshape(2, 16, half, LANES).astype(f32)
     whole = whole.transpose(1, 0, 2, 3).reshape(2 * E, LANES)

time: 154 us -> 147 us (0.955)
  starting transfers between devices: 48.3 us -> 56.8 us
  waiting for transfers between devices: 50.5 us -> 43.5 us
  blocking collectives: 39.2 us -> 34 us
  matrix products: 6.15 us -> 1.91 us
  Pallas kernels: 0 us -> 2.26 us
    ppermute x2 -> x4, starting transfers between devices: 13.3 us -> 22.3 us  [swap(): return lax.ppermute(value, axis, [(0, 1), (1, 0)])]
    all_to_all x4, waiting for transfers between devices: 44.5 us -> 38.2 us  [exchange(): return lax.all_to_all(value, axis, 0, 0, tiled=True)]
    dot_general x18 -> x2, matrix products: 4.69 us -> 0.46 us  [the longest x1 0.23 us: local(): jnp.dot(given, other_features, preferred_element_type=f32)]
    all_gather x1 -> x0, blocking collectives: 4.17 us -> none  [local(): both = lax.all_gather(weight_grad, 'core', axis=0, tiled=False)]
    all_to_all x2, blocking collectives: 31.1 us -> 28.6 us  [exchange(): return lax.all_to_all(value, axis, 0, 0, tiled=True)]
    pallas_call x0 -> x1, Pallas kernels: none -> 2.26 us  [head_partials(): pl.pallas_call(head_kernel, out_shape=jax.ShapeDtypeStruct((image_feature...]
    ppermute x3, waiting for transfers between devices: 5.38 us -> 3.25 us  [local(): lax.ppermute(column, 'x', [(i, i ^ step) for i in range(4)])]
  transfers between devices with their start and end apart: 9 -> 11, of which waited for: 7 -> 8; matrix products, arithmetic and copies ran while one was open for 1% -> 2% of each run, Pallas kernels for 0% -> 0%
where the time goes in v5:
time: 147 us; the launch traced here: 146 us
  starting transfers between devices  56.8 us (39%)
  waiting for transfers between devices  43.5 us (30%)
  blocking collectives  34 us (23%)
  local copies, waits for them, and re-layouts  4.1 us (3%)
  other arithmetic  2.29 us (2%)
  Pallas kernels  2.26 us (2%)
  matrix products  1.91 us (1%)
    all_to_all x4, waiting for transfers between devices, exchange(): return lax.all_to_all(value, axis, 0, 0, tiled=True)  38.2 us
    all_to_all x2, blocking collectives, exchange(): return lax.all_to_all(value, axis, 0, 0, tiled=True)  28.6 us
    all_to_all x4, starting transfers between devices, exchange(): return lax.all_to_all(value, axis, 0, 0, tiled=True)  25.6 us
    ppermute x4, starting transfers between devices, swap(): return lax.ppermute(value, axis, [(0, 1), (1, 0)])  22.3 us
    ppermute x3, starting transfers between devices, local(): lax.ppermute(column, 'x', [(i, i ^ step) for i in range(4)])  8.97 us
    all_gather x1, blocking collectives, local(): lax.all_gather(halves, 'core', axis=0, tiled=False)  5.44 us
    ppermute x3, waiting for transfers between devices, local(): lax.ppermute(column, 'x', [(i, i ^ step) for i in range(4)])  3.25 us
  transfers between devices with their start and end apart: 11, of which 8 were waited for; matrix products, arithmetic and copies ran while one was open for 2% of the time, Pallas kernels for 0%

profile of v5, /device:TPU:1, one launch (start us, length us, event | category | flops | bytes accessed | tf_op | source)
XLA Modules:
  0.0 145.9 jit_solution(7275179709015000945)
XLA Ops:
  0.6 2.3 %head_partials.1 = bf16[128,2560]{1,0:T(8,128)(2,1)} custom-call(bf16[96,128]{1,0:T(8,128)(2,1)} %bitcast.76, bf16[72,128]{1,0:T(8,128)(2,1)} %bitcast.77, bf16[96,1152]{1,0:T(8,128)(2,1)} %image_weight_ref.1, bf16[72,1152]{1,0:T(8,128)(2,1)} %text_weight_ref.1), custom_call_target="tpu_custom_call" | custom-call | tf_op jit(solution)/shard_map/head_partials/pallas_call | solution.py:45
  2.9 10.4 %all-to-all-start = ((bf16[16,8,2560]{2,1,0:T(8,128)(2,1)}), bf16[16,8,2560]{2,1,0:T(8,128)(2,1)S(1)}, u32[]{:S(2)}, u32[]{:S(2)}) async-start(bf16[16,8,2560]{2,1,0:T(8,128)(2,1)} %bitcast.68), calls=%async_computation | async-start | bytes 1310720 | tf_op jit(solution)/shard_map/all_to_all | solution.py:22
  13.4 15.7 %all-to-all-done = bf16[16,8,2560]{2,1,0:T(8,128)(2,1)S(1)} async-done(((bf16[16,8,2560]{2,1,0:T(8,128)(2,1)}), bf16[16,8,2560]{2,1,0:T(8,128)(2,1)S(1)}, u32[]{:S(2)}, u32[]{:S(2)}) %all-to-all-start) | async-done | bytes 655392 | tf_op jit(solution)/shard_map/all_to_all | solution.py:22
  29.6 7.9 %collective-permute-start = (bf16[8,3328]{1,0:T(8,128)(2,1)S(1)}, bf16[8,3328]{1,0:T(8,128)(2,1)S(1)}, u32[]{:S(2)}, u32[]{:S(2)}) collective-permute-start(bf16[8,3328]{1,0:T(8,128)(2,1)S(1)} %pad_maximum_fusion.3), channel_id=1, source_target_pairs={{0,256},{256,0},{1,257},{257,1},{2,258},{258,2},{3,259},{259,3},{4... | collective-permute-start | bytes 159752 | tf_op jit(solution)/shard_map/ppermute | solution.py:26
  38.3 5.0 %all-to-all-start.2 = ((bf16[8,8,1280]{2,1,0:T(8,128)(2,1)}), bf16[8,8,1280]{2,1,0:T(8,128)(2,1)S(1)}, u32[]{:S(2)}, u32[]{:S(2)}) async-start(bf16[8,8,1280]{2,1,0:T(8,128)(2,1)} %maximum_bitcast_fusion), calls=%async_computation.2 | async-start | bytes 327680 | tf_op jit(solution)/shard_map/all_to_all | solution.py:22
  43.3 8.3 %all-to-all-done.2 = bf16[8,8,1280]{2,1,0:T(8,128)(2,1)S(1)} async-done(((bf16[8,8,1280]{2,1,0:T(8,128)(2,1)}), bf16[8,8,1280]{2,1,0:T(8,128)(2,1)S(1)}, u32[]{:S(2)}, u32[]{:S(2)}) %all-to-all-start.2) | async-done | bytes 163872 | tf_op jit(solution)/shard_map/all_to_all | solution.py:22
  51.6 1.0 tile.12
  52.5 6.8 %all-to-all-start.1 = ((bf16[8,16,3328]{2,1,0:T(8,128)(2,1)}), bf16[8,16,3328]{2,1,0:T(8,128)(2,1)S(1)}, u32[]{:S(2)}, u32[]{:S(2)}) async-start(bf16[8,16,3328]{2,1,0:T(8,128)(2,1)} %tile.12), calls=%async_computation.1 | async-start | bytes 1703936 | tf_op jit(solution)/shard_map/all_to_all | solution.py:22
  59.4 2.5 %collective-permute-start.3 = (bf16[64,1280]{1,0:T(8,128)(2,1)S(1)}, bf16[64,1280]{1,0:T(8,128)(2,1)S(1)}, u32[]{:S(2)}, u32[]{:S(2)}) collective-permute-start(bf16[64,1280]{1,0:T(8,128)(2,1)S(1)} %bitcast.72), channel_id=1, source_target_pairs={{0,3},{1,2},{2,1},{3,0},{4,7},{5,6},{6,5},{7,4},{8,11},{9,10},{10,... | collective-permute-start | bytes 491528 | tf_op jit(solution)/shard_map/ppermute | solution.py:136
  61.9 3.4 %collective-permute-start.2 = (bf16[64,1280]{1,0:T(8,128)(2,1)S(1)}, bf16[64,1280]{1,0:T(8,128)(2,1)S(1)}, u32[]{:S(2)}, u32[]{:S(2)}) collective-permute-start(bf16[64,1280]{1,0:T(8,128)(2,1)S(1)} %bitcast.73), channel_id=1, source_target_pairs={{0,2},{1,3},{2,0},{3,1},{4,6},{5,7},{6,4},{7,5},{8,10},{9,11},{10,... | collective-permute-start | bytes 491528 | tf_op jit(solution)/shard_map/ppermute | solution.py:136
  65.3 3.1 %collective-permute-start.1 = (bf16[64,1280]{1,0:T(8,128)(2,1)S(1)}, bf16[64,1280]{1,0:T(8,128)(2,1)S(1)}, u32[]{:S(2)}, u32[]{:S(2)}) collective-permute-start(bf16[64,1280]{1,0:T(8,128)(2,1)S(1)} %bitcast.74), channel_id=1, source_target_pairs={{0,1},{1,0},{2,3},{3,2},{4,5},{5,4},{6,7},{7,6},{8,9},{9,8},{10,11... | collective-permute-start | bytes 491528 | tf_op jit(solution)/shard_map/ppermute | solution.py:136
  68.4 1.2 collective-permute-done.2
  69.5 2.1 %collective-permute-done.1 = bf16[64,1280]{1,0:T(8,128)(2,1)S(1)} collective-permute-done((bf16[64,1280]{1,0:T(8,128)(2,1)S(1)}, bf16[64,1280]{1,0:T(8,128)(2,1)S(1)}, u32[]{:S(2)}, u32[]{:S(2)}) %collective-permute-start.1) | collective-permute-done | bytes 163872 | tf_op jit(solution)/shard_map/ppermute | solution.py:136
  71.7 6.6 %collective-permute-start.4 = (bf16[256,1280]{1,0:T(8,128)(2,1)S(1)}, bf16[256,1280]{1,0:T(8,128)(2,1)S(1)}, u32[]{:S(2)}, u32[]{:S(2)}) collective-permute-start(bf16[256,1280]{1,0:T(8,128)(2,1)S(1)} %pad_maximum_fusion), channel_id=1, source_target_pairs={{0,16},{16,0},{1,17},{17,1},{2,18},{18,2},{3,19},{19,3},{4,20},{20... | collective-permute-start | bytes 1966088 | tf_op jit(solution)/shard_map/ppermute | solution.py:26
  78.4 1.5 %collective-permute-done.4 = bf16[256,1280]{1,0:T(8,128)(2,1)S(1)} collective-permute-done((bf16[256,1280]{1,0:T(8,128)(2,1)S(1)}, bf16[256,1280]{1,0:T(8,128)(2,1)S(1)}, u32[]{:S(2)}, u32[]{:S(2)}) %collective-permute-start.4) | collective-permute-done | bytes 655392 | tf_op jit(solution)/shard_map/ppermute | solution.py:26
  80.1 1.2 all-to-all-done.1
  83.3 5.5 %collective-permute-start.5 = (bf16[128,2048]{1,0:T(8,128)(2,1)S(1)}, bf16[128,2048]{1,0:T(8,128)(2,1)S(1)}, u32[]{:S(2)}, u32[]{:S(2)}) collective-permute-start(bf16[128,2048]{1,0:T(8,128)(2,1)S(1)} %slice.117), channel_id=1, source_target_pairs={{0,16},{16,0},{1,17},{17,1},{2,18},{18,2},{3,19},{19,3},{4,20},{20... | collective-permute-start | bytes 1572872 | tf_op jit(solution)/shard_map/ppermute | solution.py:26
  89.6 3.4 %all-to-all-start.3 = ((bf16[8,144,128]{2,1,0:T(8,128)(2,1)}), bf16[8,144,128]{2,1,0:T(8,128)(2,1)S(1)}, u32[]{:S(2)}, u32[]{:S(2)}) async-start(bf16[8,144,128]{2,1,0:T(8,128)(2,1)} %bitcast.19), calls=%async_computation.3 | async-start | bytes 589824 | tf_op jit(solution)/shard_map/all_to_all | solution.py:22
  93.1 13.0 %all-to-all-done.3 = bf16[8,144,128]{2,1,0:T(8,128)(2,1)S(1)} async-done(((bf16[8,144,128]{2,1,0:T(8,128)(2,1)}), bf16[8,144,128]{2,1,0:T(8,128)(2,1)S(1)}, u32[]{:S(2)}, u32[]{:S(2)}) %all-to-all-start.3) | async-done | bytes 294944 | tf_op jit(solution)/shard_map/all_to_all | solution.py:22
  106.1 2.3 %collective-permute-start.6 = (bf16[72,128]{1,0:T(8,128)(2,1)S(1)}, bf16[72,128]{1,0:T(8,128)(2,1)S(1)}, u32[]{:S(2)}, u32[]{:S(2)}) collective-permute-start(bf16[72,128]{1,0:T(8,128)(2,1)S(1)} %broadcast_select_fusion.4), channel_id=1, source_target_pairs={{0,16},{16,0},{1,17},{17,1},{2,18},{18,2},{3,19},{19,3},{4,20},{20... | collective-permute-start | bytes 55304 | tf_op jit(solution)/shard_map/ppermute | solution.py:26
  109.6 13.3 %all_to_all.57 = bf16[16,72,128]{2,1,0:T(8,128)(2,1)S(1)} all-to-all(bf16[16,72,128]{2,1,0:T(8,128)(2,1)S(1)} %bitcast.71), channel_id=1, replica_groups=mesh['zh'=2,'y'=8,'core'=2,'zl'=4,'x'=4] {'zl','x'}, dimensions={0} | all-to-all | bytes 589824 | tf_op jit(solution)/shard_map/all_to_all | solution.py:22
  123.0 15.3 %all_to_all.58 = bf16[16,72,128]{2,1,0:T(8,128)(2,1)S(1)} all-to-all(bf16[16,72,128]{2,1,0:T(8,128)(2,1)S(1)} %tile.17), channel_id=1, replica_groups=mesh['zh'=2,'y'=8,'core'=2,'zl'=4,'x'=4] {'zh','y'}, dimensions={0} | all-to-all | bytes 589824 | tf_op jit(solution)/shard_map/all_to_all | solution.py:22
  138.3 5.4 %all_gather.7 = bf16[2,1152,128]{2,1,0:T(8,128)(2,1)S(1)} all-gather(bf16[1,1152,128]{2,1,0:T(8,128)(2,1)S(1)} %bitcast.70), channel_id=1, replica_groups=mesh['zh'=2,'y'=8,'core'=2,'zl'=4,'x'=4] {'core'}, dimensions={0}, use_global_device_ids=true | all-gather | bytes 884736 | tf_op jit(solution)/shard_map/all_gather | solution.py:157
  144.0 1.0 copy.20
  (48 shorter events, 6.9 us)
Async XLA Ops:
  0.6 12.7 %copy-start = (s32[128]{0:T(128)S(1)}, s32[128]{0:T(128)}, u32[]{:S(2)}) copy-start(s32[128]{0:T(128)} %param.9) | copy-start | bytes 1540
  2.9 26.3 %all-to-all-start = ((bf16[16,8,2560]{2,1,0:T(8,128)(2,1)}), bf16[16,8,2560]{2,1,0:T(8,128)(2,1)S(1)}, u32[]{:S(2)}, u32[]{:S(2)}) async-start(bf16[16,8,2560]{2,1,0:T(8,128)(2,1)} %bitcast.68), calls=%async_computation | async-start | bytes 1310720 | tf_op jit(solution)/shard_map/all_to_all | solution.py:22
  29.6 13.6 %collective-permute-start = (bf16[8,3328]{1,0:T(8,128)(2,1)S(1)}, bf16[8,3328]{1,0:T(8,128)(2,1)S(1)}, u32[]{:S(2)}, u32[]{:S(2)}) collective-permute-start(bf16[8,3328]{1,0:T(8,128)(2,1)S(1)} %pad_maximum_fusion.3), channel_id=1, source_target_pairs={{0,256},{256,0},{1,257},{257,1},{2,258},{258,2},{3,259},{259,3},{4... | collective-permute-start | bytes 159752 | tf_op jit(solution)/shard_map/ppermute | solution.py:26
  38.3 13.3 %all-to-all-start.2 = ((bf16[8,8,1280]{2,1,0:T(8,128)(2,1)}), bf16[8,8,1280]{2,1,0:T(8,128)(2,1)S(1)}, u32[]{:S(2)}, u32[]{:S(2)}) async-start(bf16[8,8,1280]{2,1,0:T(8,128)(2,1)} %maximum_bitcast_fusion), calls=%async_computation.2 | async-start | bytes 327680 | tf_op jit(solution)/shard_map/all_to_all | solution.py:22
  52.5 28.8 %all-to-all-start.1 = ((bf16[8,16,3328]{2,1,0:T(8,128)(2,1)}), bf16[8,16,3328]{2,1,0:T(8,128)(2,1)S(1)}, u32[]{:S(2)}, u32[]{:S(2)}) async-start(bf16[8,16,3328]{2,1,0:T(8,128)(2,1)} %tile.12), calls=%async_computation.1 | async-start | bytes 1703936 | tf_op jit(solution)/shard_map/all_to_all | solution.py:22
  59.4 9.0 %collective-permute-start.3 = (bf16[64,1280]{1,0:T(8,128)(2,1)S(1)}, bf16[64,1280]{1,0:T(8,128)(2,1)S(1)}, u32[]{:S(2)}, u32[]{:S(2)}) collective-permute-start(bf16[64,1280]{1,0:T(8,128)(2,1)S(1)} %bitcast.72), channel_id=1, source_target_pairs={{0,3},{1,2},{2,1},{3,0},{4,7},{5,6},{6,5},{7,4},{8,11},{9,10},{10,... | collective-permute-start | bytes 491528 | tf_op jit(solution)/shard_map/ppermute | solution.py:136
  61.9 7.7 %collective-permute-start.2 = (bf16[64,1280]{1,0:T(8,128)(2,1)S(1)}, bf16[64,1280]{1,0:T(8,128)(2,1)S(1)}, u32[]{:S(2)}, u32[]{:S(2)}) collective-permute-start(bf16[64,1280]{1,0:T(8,128)(2,1)S(1)} %bitcast.73), channel_id=1, source_target_pairs={{0,2},{1,3},{2,0},{3,1},{4,6},{5,7},{6,4},{7,5},{8,10},{9,11},{10,... | collective-permute-start | bytes 491528 | tf_op jit(solution)/shard_map/ppermute | solution.py:136
  65.3 6.4 %collective-permute-start.1 = (bf16[64,1280]{1,0:T(8,128)(2,1)S(1)}, bf16[64,1280]{1,0:T(8,128)(2,1)S(1)}, u32[]{:S(2)}, u32[]{:S(2)}) collective-permute-start(bf16[64,1280]{1,0:T(8,128)(2,1)S(1)} %bitcast.74), channel_id=1, source_target_pairs={{0,1},{1,0},{2,3},{3,2},{4,5},{5,4},{6,7},{7,6},{8,9},{9,8},{10,11... | collective-permute-start | bytes 491528 | tf_op jit(solution)/shard_map/ppermute | solution.py:136
  71.7 8.3 %collective-permute-start.4 = (bf16[256,1280]{1,0:T(8,128)(2,1)S(1)}, bf16[256,1280]{1,0:T(8,128)(2,1)S(1)}, u32[]{:S(2)}, u32[]{:S(2)}) collective-permute-start(bf16[256,1280]{1,0:T(8,128)(2,1)S(1)} %pad_maximum_fusion), channel_id=1, source_target_pairs={{0,16},{16,0},{1,17},{17,1},{2,18},{18,2},{3,19},{19,3},{4,20},{20... | collective-permute-start | bytes 1966088 | tf_op jit(solution)/shard_map/ppermute | solution.py:26
  83.3 22.8 %collective-permute-start.5 = (bf16[128,2048]{1,0:T(8,128)(2,1)S(1)}, bf16[128,2048]{1,0:T(8,128)(2,1)S(1)}, u32[]{:S(2)}, u32[]{:S(2)}) collective-permute-start(bf16[128,2048]{1,0:T(8,128)(2,1)S(1)} %slice.117), channel_id=1, source_target_pairs={{0,16},{16,0},{1,17},{17,1},{2,18},{18,2},{3,19},{19,3},{4,20},{20... | collective-permute-start | bytes 1572872 | tf_op jit(solution)/shard_map/ppermute | solution.py:26
  89.6 16.4 %all-to-all-start.3 = ((bf16[8,144,128]{2,1,0:T(8,128)(2,1)}), bf16[8,144,128]{2,1,0:T(8,128)(2,1)S(1)}, u32[]{:S(2)}, u32[]{:S(2)}) async-start(bf16[8,144,128]{2,1,0:T(8,128)(2,1)} %bitcast.19), calls=%async_computation.3 | async-start | bytes 589824 | tf_op jit(solution)/shard_map/all_to_all | solution.py:22
  106.1 3.2 %collective-permute-start.6 = (bf16[72,128]{1,0:T(8,128)(2,1)S(1)}, bf16[72,128]{1,0:T(8,128)(2,1)S(1)}, u32[]{:S(2)}, u32[]{:S(2)}) collective-permute-start(bf16[72,128]{1,0:T(8,128)(2,1)S(1)} %broadcast_select_fusion.4), channel_id=1, source_target_pairs={{0,16},{16,0},{1,17},{17,1},{2,18},{18,2},{3,19},{19,3},{4,20},{20... | collective-permute-start | bytes 55304 | tf_op jit(solution)/shard_map/ppermute | solution.py:26

commit v6 on v5

--- a/solution.py
+++ b/solution.py
@@ -139,17 +139,15 @@
     terms = grad_terms(n1, [block, swap(block, "core")])
 
     features = n1[:, E + LANES :]
-    terms, features = lax.optimization_barrier((terms, features))
-    other_features = swap(features, "core")
     chunk = E // 8
     half = chunk // 2
-    core = lax.axis_index("core")
-    parts, other_features = lax.optimization_barrier((exchange(terms, "y"), other_features))
+    terms, features, core = lax.optimization_barrier((terms, features, lax.axis_index("core")))
+    parts, features, core = lax.optimization_barrier((exchange(terms, "y"), features, core))
     dpre = jnp.sum(parts.astype(f32).reshape(8, chunk, -1), axis=0).astype(bf16)
     kept = jnp.where(core == 0, dpre[:half], dpre[half:])
-    given = swap(jnp.where(core == 0, dpre[half:], dpre[:half]), "core")
-    weight_grad = jnp.dot(kept, features, preferred_element_type=f32)
-    weight_grad = weight_grad + jnp.dot(given, other_features, preferred_element_type=f32)
+    given = jnp.where(core == 0, dpre[half:], dpre[:half])
+    given = swap(jnp.dot(given, features, preferred_element_type=f32).astype(bf16), "core")
+    weight_grad = jnp.dot(kept, features, preferred_element_type=f32) + given.astype(f32)
     parts = weight_grad.astype(bf16).reshape(half, 16, LANES).transpose(1, 0, 2).reshape(16 * half, LANES)
     parts = exchange(parts, TXT).astype(f32).reshape(16, half, LANES)
     weight_grad = jnp.sum(parts, axis=0).astype(bf16)

time: 147 us -> 144 us (0.980)
  blocking collectives: 34 us -> 52.5 us
  waiting for transfers between devices: 43.5 us -> 31.1 us
  starting transfers between devices: 56.8 us -> 48.9 us
    all_to_all x2 -> x3, blocking collectives: 28.6 us -> 47.1 us  [exchange(): return lax.all_to_all(value, axis, 0, 0, tiled=True)]
    all_to_all x4 -> x3, waiting for transfers between devices: 38.2 us -> 25.2 us  [exchange(): return lax.all_to_all(value, axis, 0, 0, tiled=True)]
    ppermute x4 -> x3, starting transfers between devices: 22.3 us -> 17.8 us  [swap(): return lax.ppermute(value, axis, [(0, 1), (1, 0)])]
    all_to_all x4 -> x3, starting transfers between devices: 25.6 us -> 22.2 us  [exchange(): return lax.all_to_all(value, axis, 0, 0, tiled=True)]
  transfers between devices with their start and end apart: 11 -> 9, of which waited for: 8 -> 7; matrix products, arithmetic and copies ran while one was open for 2% -> 1% of each run, Pallas kernels for 0% -> 0%
where the time goes in v6:
time: 144 us; the launch traced here: 143 us
  blocking collectives  52.5 us (36%)
  starting transfers between devices  48.9 us (34%)
  waiting for transfers between devices  31.1 us (22%)
  local copies, waits for them, and re-layouts  3.42 us (2%)
  other arithmetic  2.28 us (2%)
  Pallas kernels  2.25 us (2%)
  matrix products  1.91 us (1%)
    all_to_all x3, blocking collectives, exchange(): return lax.all_to_all(value, axis, 0, 0, tiled=True)  47.1 us
    all_to_all x3, waiting for transfers between devices, exchange(): return lax.all_to_all(value, axis, 0, 0, tiled=True)  25.2 us
    all_to_all x3, starting transfers between devices, exchange(): return lax.all_to_all(value, axis, 0, 0, tiled=True)  22.2 us
    ppermute x3, starting transfers between devices, swap(): return lax.ppermute(value, axis, [(0, 1), (1, 0)])  17.8 us
    ppermute x3, starting transfers between devices, local(): lax.ppermute(column, 'x', [(i, i ^ step) for i in range(4)])  8.97 us
    all_gather x1, blocking collectives, local(): lax.all_gather(halves, 'core', axis=0, tiled=False)  5.46 us
    ppermute x3, waiting for transfers between devices, local(): lax.ppermute(column, 'x', [(i, i ^ step) for i in range(4)])  3.25 us
  transfers between devices with their start and end apart: 9, of which 7 were waited for; matrix products, arithmetic and copies ran while one was open for 1% of the time, Pallas kernels for 0%

profile of v6, /device:TPU:1, one launch (start us, length us, event | category | flops | bytes accessed | tf_op | source)
XLA Modules:
  0.0 143.3 jit_solution(13900899946490224733)
XLA Ops:
  0.6 2.3 %head_partials.1 = bf16[128,2560]{1,0:T(8,128)(2,1)} custom-call(bf16[96,128]{1,0:T(8,128)(2,1)} %bitcast.76, bf16[72,128]{1,0:T(8,128)(2,1)} %bitcast.77, bf16[96,1152]{1,0:T(8,128)(2,1)} %image_weight_ref.1, bf16[72,1152]{1,0:T(8,128)(2,1)} %text_weight_ref.1), custom_call_target="tpu_custom_call" | custom-call | tf_op jit(solution)/shard_map/head_partials/pallas_call | solution.py:45
  2.9 10.4 %all-to-all-start = ((bf16[16,8,2560]{2,1,0:T(8,128)(2,1)}), bf16[16,8,2560]{2,1,0:T(8,128)(2,1)S(1)}, u32[]{:S(2)}, u32[]{:S(2)}) async-start(bf16[16,8,2560]{2,1,0:T(8,128)(2,1)} %bitcast.67), calls=%async_computation | async-start | bytes 1310720 | tf_op jit(solution)/shard_map/all_to_all | solution.py:22
  13.4 15.7 %all-to-all-done = bf16[16,8,2560]{2,1,0:T(8,128)(2,1)S(1)} async-done(((bf16[16,8,2560]{2,1,0:T(8,128)(2,1)}), bf16[16,8,2560]{2,1,0:T(8,128)(2,1)S(1)}, u32[]{:S(2)}, u32[]{:S(2)}) %all-to-all-start) | async-done | bytes 655392 | tf_op jit(solution)/shard_map/all_to_all | solution.py:22
  29.6 7.9 %collective-permute-start = (bf16[8,3328]{1,0:T(8,128)(2,1)S(1)}, bf16[8,3328]{1,0:T(8,128)(2,1)S(1)}, u32[]{:S(2)}, u32[]{:S(2)}) collective-permute-start(bf16[8,3328]{1,0:T(8,128)(2,1)S(1)} %pad_maximum_fusion.3), channel_id=1, source_target_pairs={{0,256},{256,0},{1,257},{257,1},{2,258},{258,2},{3,259},{259,3},{4... | collective-permute-start | bytes 159752 | tf_op jit(solution)/shard_map/ppermute | solution.py:26
  38.3 5.0 %all-to-all-start.2 = ((bf16[8,8,1280]{2,1,0:T(8,128)(2,1)}), bf16[8,8,1280]{2,1,0:T(8,128)(2,1)S(1)}, u32[]{:S(2)}, u32[]{:S(2)}) async-start(bf16[8,8,1280]{2,1,0:T(8,128)(2,1)} %maximum_bitcast_fusion), calls=%async_computation.2 | async-start | bytes 327680 | tf_op jit(solution)/shard_map/all_to_all | solution.py:22
  43.3 8.3 %all-to-all-done.2 = bf16[8,8,1280]{2,1,0:T(8,128)(2,1)S(1)} async-done(((bf16[8,8,1280]{2,1,0:T(8,128)(2,1)}), bf16[8,8,1280]{2,1,0:T(8,128)(2,1)S(1)}, u32[]{:S(2)}, u32[]{:S(2)}) %all-to-all-start.2) | async-done | bytes 163872 | tf_op jit(solution)/shard_map/all_to_all | solution.py:22
  51.6 1.0 tile.12
  52.5 6.8 %all-to-all-start.1 = ((bf16[8,16,3328]{2,1,0:T(8,128)(2,1)}), bf16[8,16,3328]{2,1,0:T(8,128)(2,1)S(1)}, u32[]{:S(2)}, u32[]{:S(2)}) async-start(bf16[8,16,3328]{2,1,0:T(8,128)(2,1)} %tile.12), calls=%async_computation.1 | async-start | bytes 1703936 | tf_op jit(solution)/shard_map/all_to_all | solution.py:22
  59.3 2.5 %collective-permute-start.3 = (bf16[64,1280]{1,0:T(8,128)(2,1)S(1)}, bf16[64,1280]{1,0:T(8,128)(2,1)S(1)}, u32[]{:S(2)}, u32[]{:S(2)}) collective-permute-start(bf16[64,1280]{1,0:T(8,128)(2,1)S(1)} %bitcast.72), channel_id=1, source_target_pairs={{0,3},{1,2},{2,1},{3,0},{4,7},{5,6},{6,5},{7,4},{8,11},{9,10},{10,... | collective-permute-start | bytes 491528 | tf_op jit(solution)/shard_map/ppermute | solution.py:136
  61.9 3.4 %collective-permute-start.2 = (bf16[64,1280]{1,0:T(8,128)(2,1)S(1)}, bf16[64,1280]{1,0:T(8,128)(2,1)S(1)}, u32[]{:S(2)}, u32[]{:S(2)}) collective-permute-start(bf16[64,1280]{1,0:T(8,128)(2,1)S(1)} %bitcast.73), channel_id=1, source_target_pairs={{0,2},{1,3},{2,0},{3,1},{4,6},{5,7},{6,4},{7,5},{8,10},{9,11},{10,... | collective-permute-start | bytes 491528 | tf_op jit(solution)/shard_map/ppermute | solution.py:136
  65.2 3.1 %collective-permute-start.1 = (bf16[64,1280]{1,0:T(8,128)(2,1)S(1)}, bf16[64,1280]{1,0:T(8,128)(2,1)S(1)}, u32[]{:S(2)}, u32[]{:S(2)}) collective-permute-start(bf16[64,1280]{1,0:T(8,128)(2,1)S(1)} %bitcast.74), channel_id=1, source_target_pairs={{0,1},{1,0},{2,3},{3,2},{4,5},{5,4},{6,7},{7,6},{8,9},{9,8},{10,11... | collective-permute-start | bytes 491528 | tf_op jit(solution)/shard_map/ppermute | solution.py:136
  68.3 1.2 collective-permute-done.2
  69.5 2.1 %collective-permute-done.1 = bf16[64,1280]{1,0:T(8,128)(2,1)S(1)} collective-permute-done((bf16[64,1280]{1,0:T(8,128)(2,1)S(1)}, bf16[64,1280]{1,0:T(8,128)(2,1)S(1)}, u32[]{:S(2)}, u32[]{:S(2)}) %collective-permute-start.1) | collective-permute-done | bytes 163872 | tf_op jit(solution)/shard_map/ppermute | solution.py:136
  71.6 6.6 %collective-permute-start.4 = (bf16[256,1280]{1,0:T(8,128)(2,1)S(1)}, bf16[256,1280]{1,0:T(8,128)(2,1)S(1)}, u32[]{:S(2)}, u32[]{:S(2)}) collective-permute-start(bf16[256,1280]{1,0:T(8,128)(2,1)S(1)} %pad_maximum_fusion), channel_id=1, source_target_pairs={{0,16},{16,0},{1,17},{17,1},{2,18},{18,2},{3,19},{19,3},{4,20},{20... | collective-permute-start | bytes 1966088 | tf_op jit(solution)/shard_map/ppermute | solution.py:26
  78.4 1.5 %collective-permute-done.4 = bf16[256,1280]{1,0:T(8,128)(2,1)S(1)} collective-permute-done((bf16[256,1280]{1,0:T(8,128)(2,1)S(1)}, bf16[256,1280]{1,0:T(8,128)(2,1)S(1)}, u32[]{:S(2)}, u32[]{:S(2)}) %collective-permute-start.4) | collective-permute-done | bytes 655392 | tf_op jit(solution)/shard_map/ppermute | solution.py:26
  80.1 1.2 all-to-all-done.1
  83.5 17.7 %all_to_all.57 = bf16[8,144,128]{2,1,0:T(8,128)(2,1)S(1)} all-to-all(bf16[8,144,128]{2,1,0:T(8,128)(2,1)S(1)} %bitcast.70), channel_id=1, replica_groups=mesh['zh'=2,'y'=8,'core'=2,'zl'=4,'x'=4] {'y'}, dimensions={0} | all-to-all | bytes 589824 | tf_op jit(solution)/shard_map/all_to_all | solution.py:22
  101.5 3.3 %collective-permute-start.5 = (bf16[72,2048]{1,0:T(8,128)(2,1)S(1)}, bf16[72,2048]{1,0:T(8,128)(2,1)S(1)}, u32[]{:S(2)}, u32[]{:S(2)}) collective-permute-start(bf16[72,2048]{1,0:T(8,128)(2,1)S(1)} %convolution_convert_fusion), channel_id=1, source_target_pairs={{0,16},{16,0},{1,17},{17,1},{2,18},{18,2},{3,19},{19,3},{4,20},{20... | collective-permute-start | bytes 884744 | tf_op jit(solution)/shard_map/ppermute | solution.py:26
  104.7 1.2 collective-permute-done.5
  106.2 13.4 %all_to_all.58 = bf16[16,72,128]{2,1,0:T(8,128)(2,1)S(1)} all-to-all(bf16[16,72,128]{2,1,0:T(8,128)(2,1)S(1)} %bitcast.71), channel_id=1, replica_groups=mesh['zh'=2,'y'=8,'core'=2,'zl'=4,'x'=4] {'zl','x'}, dimensions={0} | all-to-all | bytes 589824 | tf_op jit(solution)/shard_map/all_to_all | solution.py:22
  119.7 15.9 %all_to_all.59 = bf16[16,72,128]{2,1,0:T(8,128)(2,1)S(1)} all-to-all(bf16[16,72,128]{2,1,0:T(8,128)(2,1)S(1)} %tile.17), channel_id=1, replica_groups=mesh['zh'=2,'y'=8,'core'=2,'zl'=4,'x'=4] {'zh','y'}, dimensions={0} | all-to-all | bytes 589824 | tf_op jit(solution)/shard_map/all_to_all | solution.py:22
  135.7 5.5 %all_gather.7 = bf16[2,1152,128]{2,1,0:T(8,128)(2,1)S(1)} all-gather(bf16[1,1152,128]{2,1,0:T(8,128)(2,1)S(1)} %bitcast.69), channel_id=1, replica_groups=mesh['zh'=2,'y'=8,'core'=2,'zl'=4,'x'=4] {'core'}, dimensions={0}, use_global_device_ids=true | all-gather | bytes 884736 | tf_op jit(solution)/shard_map/all_gather | solution.py:155
  141.4 1.0 copy.20
  142.4 0.9 copy.21
  (44 shorter events, 4.7 us)
Async XLA Ops:
  0.6 12.7 %copy-start = (s32[128]{0:T(128)S(1)}, s32[128]{0:T(128)}, u32[]{:S(2)}) copy-start(s32[128]{0:T(128)} %param.9) | copy-start | bytes 1540
  2.9 26.3 %all-to-all-start = ((bf16[16,8,2560]{2,1,0:T(8,128)(2,1)}), bf16[16,8,2560]{2,1,0:T(8,128)(2,1)S(1)}, u32[]{:S(2)}, u32[]{:S(2)}) async-start(bf16[16,8,2560]{2,1,0:T(8,128)(2,1)} %bitcast.67), calls=%async_computation | async-start | bytes 1310720 | tf_op jit(solution)/shard_map/all_to_all | solution.py:22
  29.6 13.6 %collective-permute-start = (bf16[8,3328]{1,0:T(8,128)(2,1)S(1)}, bf16[8,3328]{1,0:T(8,128)(2,1)S(1)}, u32[]{:S(2)}, u32[]{:S(2)}) collective-permute-start(bf16[8,3328]{1,0:T(8,128)(2,1)S(1)} %pad_maximum_fusion.3), channel_id=1, source_target_pairs={{0,256},{256,0},{1,257},{257,1},{2,258},{258,2},{3,259},{259,3},{4... | collective-permute-start | bytes 159752 | tf_op jit(solution)/shard_map/ppermute | solution.py:26
  38.3 13.3 %all-to-all-start.2 = ((bf16[8,8,1280]{2,1,0:T(8,128)(2,1)}), bf16[8,8,1280]{2,1,0:T(8,128)(2,1)S(1)}, u32[]{:S(2)}, u32[]{:S(2)}) async-start(bf16[8,8,1280]{2,1,0:T(8,128)(2,1)} %maximum_bitcast_fusion), calls=%async_computation.2 | async-start | bytes 327680 | tf_op jit(solution)/shard_map/all_to_all | solution.py:22
  52.5 28.8 %all-to-all-start.1 = ((bf16[8,16,3328]{2,1,0:T(8,128)(2,1)}), bf16[8,16,3328]{2,1,0:T(8,128)(2,1)S(1)}, u32[]{:S(2)}, u32[]{:S(2)}) async-start(bf16[8,16,3328]{2,1,0:T(8,128)(2,1)} %tile.12), calls=%async_computation.1 | async-start | bytes 1703936 | tf_op jit(solution)/shard_map/all_to_all | solution.py:22
  59.3 9.0 %collective-permute-start.3 = (bf16[64,1280]{1,0:T(8,128)(2,1)S(1)}, bf16[64,1280]{1,0:T(8,128)(2,1)S(1)}, u32[]{:S(2)}, u32[]{:S(2)}) collective-permute-start(bf16[64,1280]{1,0:T(8,128)(2,1)S(1)} %bitcast.72), channel_id=1, source_target_pairs={{0,3},{1,2},{2,1},{3,0},{4,7},{5,6},{6,5},{7,4},{8,11},{9,10},{10,... | collective-permute-start | bytes 491528 | tf_op jit(solution)/shard_map/ppermute | solution.py:136
  61.9 7.7 %collective-permute-start.2 = (bf16[64,1280]{1,0:T(8,128)(2,1)S(1)}, bf16[64,1280]{1,0:T(8,128)(2,1)S(1)}, u32[]{:S(2)}, u32[]{:S(2)}) collective-permute-start(bf16[64,1280]{1,0:T(8,128)(2,1)S(1)} %bitcast.73), channel_id=1, source_target_pairs={{0,2},{1,3},{2,0},{3,1},{4,6},{5,7},{6,4},{7,5},{8,10},{9,11},{10,... | collective-permute-start | bytes 491528 | tf_op jit(solution)/shard_map/ppermute | solution.py:136
  65.2 6.4 %collective-permute-start.1 = (bf16[64,1280]{1,0:T(8,128)(2,1)S(1)}, bf16[64,1280]{1,0:T(8,128)(2,1)S(1)}, u32[]{:S(2)}, u32[]{:S(2)}) collective-permute-start(bf16[64,1280]{1,0:T(8,128)(2,1)S(1)} %bitcast.74), channel_id=1, source_target_pairs={{0,1},{1,0},{2,3},{3,2},{4,5},{5,4},{6,7},{7,6},{8,9},{9,8},{10,11... | collective-permute-start | bytes 491528 | tf_op jit(solution)/shard_map/ppermute | solution.py:136
  71.6 8.3 %collective-permute-start.4 = (bf16[256,1280]{1,0:T(8,128)(2,1)S(1)}, bf16[256,1280]{1,0:T(8,128)(2,1)S(1)}, u32[]{:S(2)}, u32[]{:S(2)}) collective-permute-start(bf16[256,1280]{1,0:T(8,128)(2,1)S(1)} %pad_maximum_fusion), channel_id=1, source_target_pairs={{0,16},{16,0},{1,17},{17,1},{2,18},{18,2},{3,19},{19,3},{4,20},{20... | collective-permute-start | bytes 1966088 | tf_op jit(solution)/shard_map/ppermute | solution.py:26
  101.5 4.5 %collective-permute-start.5 = (bf16[72,2048]{1,0:T(8,128)(2,1)S(1)}, bf16[72,2048]{1,0:T(8,128)(2,1)S(1)}, u32[]{:S(2)}, u32[]{:S(2)}) collective-permute-start(bf16[72,2048]{1,0:T(8,128)(2,1)S(1)} %convolution_convert_fusion), channel_id=1, source_target_pairs={{0,16},{16,0},{1,17},{17,1},{2,18},{18,2},{3,19},{19,3},{4,20},{20... | collective-permute-start | bytes 884744 | tf_op jit(solution)/shard_map/ppermute | solution.py:26

commit v7 on v6

--- a/solution.py
+++ b/solution.py
@@ -10,6 +10,7 @@
 EPS = 1e-06
 E = 1152
 LANES = 128
+SPARE = 96
 AXES = ("zh", "y", "core", "zl", "x")
 IMG = ("zh", "y", "core")
 ZY = ("zh", "y")
@@ -49,11 +50,11 @@
     )(image_features.T, text_features.T, image_weight, text_weight)
 
 
-def columns_in_lanes(columns, rows):
+def columns_in_lanes(columns, rows, first=0):
     lane = lax.broadcasted_iota(jnp.int32, (rows, LANES), 1)
     lanes = jnp.zeros((rows, LANES), f32)
     for place, column in enumerate(columns):
-        lanes = jnp.where(lane == place, column, lanes)
+        lanes = jnp.where(lane == first + place, column, lanes)
     return lanes
 
 
@@ -75,9 +76,9 @@
         pre = total[:, tower * E : (tower + 1) * E]
         scale = lax.rsqrt(jnp.sum(pre * pre, -1, keepdims=True) + EPS)
         unit = pre * scale
-        extra1 = columns_in_lanes(key_digits(key1) + hi_lo(scale), rows)
+        extra1 = columns_in_lanes(key_digits(key1) + hi_lo(scale), rows, SPARE)
         extra2 = columns_in_lanes(key_digits(key2), rows)
-        first.append(jnp.concatenate([unit, extra1], axis=1).astype(bf16))
+        first.append((unit.astype(bf16), extra1.astype(bf16)))
         second.append(jnp.concatenate([unit, extra2], axis=1).astype(bf16))
     return first, second
 
@@ -85,8 +86,8 @@
 def grad_terms(n1, n2_blocks):
     rows = n1.shape[0]
     info = n1[:, E : E + LANES].astype(f32)
-    key1 = info[:, 0:1] * 64.0 + info[:, 1:2]
-    scale = info[:, 2:3] + info[:, 3:4]
+    key1 = info[:, SPARE : SPARE + 1] * 64.0 + info[:, SPARE + 1 : SPARE + 2]
+    scale = info[:, SPARE + 2 : SPARE + 3] + info[:, SPARE + 3 : SPARE + 4]
     unit = n1[:, :E]
     grad = jnp.zeros((rows, E), f32)
     for block in n2_blocks:
@@ -121,15 +122,15 @@
         part = partials[:, 2 * E + tower * LANES : 2 * E + (tower + 1) * LANES]
         return part.reshape(16, own_rows, LANES).transpose(1, 0, 2).reshape(own_rows, 16 * LANES)
 
-    features = [all_features(0), all_features(1)]
     pairs = lax.dynamic_slice_in_dim(pair_index, txt * own_rows, own_rows, 0).astype(f32)[:, None]
     ids = (img * block_rows + txt * own_rows + jnp.arange(own_rows)).astype(f32)[:, None]
     first, second = unit_rows(partials, pairs, ids)
+    for tower, (unit, extra) in enumerate(first):
+        lanes = all_features(tower)
+        first[tower] = jnp.concatenate([unit, lanes[:, :LANES] + extra, lanes[:, LANES:]], axis=1)
 
     n1_own, n1_given = pick(*first), pick(*first[::-1])
-    x_own, x_given = pick(*features), pick(*features[::-1])
-    n1_own = jnp.concatenate([n1_own, x_own], axis=1)
-    given = swap(jnp.concatenate([n1_given, x_given], axis=1), "zh")
+    given = swap(n1_given, "zh")
     n1_own = jnp.concatenate([pick(n1_own, given), pick(given, n1_own)], axis=0)
 
     column = exchange(jnp.concatenate([jnp.tile(second[1], (4, 1)), jnp.tile(second[0], (4, 1))], axis=0), ("zh", "zl"))
@@ -138,7 +139,7 @@
     n1 = exchange(jnp.tile(n1_own, (8, 1)), "y")
     terms = grad_terms(n1, [block, swap(block, "core")])
 
-    features = n1[:, E + LANES :]
+    features = n1[:, E:]
     chunk = E // 8
     half = chunk // 2
     terms, features, core = lax.optimization_barrier((terms, features, lax.axis_index("core")))

time: 144 us -> 144 us (level)
  no operation moved by 1% of the time
where the time goes in v7:
time: 144 us; the launch traced here: 143 us
  blocking collectives  53.3 us (37%)
  starting transfers between devices  48.9 us (34%)
  waiting for transfers between devices  30.4 us (21%)
  local copies, waits for them, and re-layouts  3.42 us (2%)
  other arithmetic  2.3 us (2%)
  Pallas kernels  2.25 us (2%)
  matrix products  1.91 us (1%)
    all_to_all x3, blocking collectives, exchange(): return lax.all_to_all(value, axis, 0, 0, tiled=True)  47.8 us
    all_to_all x3, waiting for transfers between devices, exchange(): return lax.all_to_all(value, axis, 0, 0, tiled=True)  24.4 us
    all_to_all x3, starting transfers between devices, exchange(): return lax.all_to_all(value, axis, 0, 0, tiled=True)  22.2 us
    ppermute x3, starting transfers between devices, swap(): return lax.ppermute(value, axis, [(0, 1), (1, 0)])  17.7 us
    ppermute x3, starting transfers between devices, local(): lax.ppermute(column, 'x', [(i, i ^ step) for i in range(4)])  8.97 us
    all_gather x1, blocking collectives, local(): lax.all_gather(halves, 'core', axis=0, tiled=False)  5.46 us
    ppermute x3, waiting for transfers between devices, local(): lax.ppermute(column, 'x', [(i, i ^ step) for i in range(4)])  3.25 us
  transfers between devices with their start and end apart: 9, of which 7 were waited for; matrix products, arithmetic and copies ran while one was open for 1% of the time, Pallas kernels for 0%

profile of v7, /device:TPU:1, one launch (start us, length us, event | category | flops | bytes accessed | tf_op | source)
XLA Modules:
  0.0 143.4 jit_solution(3919240855001635992)
XLA Ops:
  0.6 2.3 %head_partials.1 = bf16[128,2560]{1,0:T(8,128)(2,1)} custom-call(bf16[96,128]{1,0:T(8,128)(2,1)} %bitcast.76, bf16[72,128]{1,0:T(8,128)(2,1)} %bitcast.77, bf16[96,1152]{1,0:T(8,128)(2,1)} %image_weight_ref.1, bf16[72,1152]{1,0:T(8,128)(2,1)} %text_weight_ref.1), custom_call_target="tpu_custom_call" | custom-call | tf_op jit(solution)/shard_map/head_partials/pallas_call | solution.py:46
  2.9 10.4 %all-to-all-start = ((bf16[16,8,2560]{2,1,0:T(8,128)(2,1)}), bf16[16,8,2560]{2,1,0:T(8,128)(2,1)S(1)}, u32[]{:S(2)}, u32[]{:S(2)}) async-start(bf16[16,8,2560]{2,1,0:T(8,128)(2,1)} %bitcast.67), calls=%async_computation | async-start | bytes 1310720 | tf_op jit(solution)/shard_map/all_to_all | solution.py:23
  13.4 15.7 %all-to-all-done = bf16[16,8,2560]{2,1,0:T(8,128)(2,1)S(1)} async-done(((bf16[16,8,2560]{2,1,0:T(8,128)(2,1)}), bf16[16,8,2560]{2,1,0:T(8,128)(2,1)S(1)}, u32[]{:S(2)}, u32[]{:S(2)}) %all-to-all-start) | async-done | bytes 655392 | tf_op jit(solution)/shard_map/all_to_all | solution.py:23
  29.6 7.9 %collective-permute-start = (bf16[8,3200]{1,0:T(8,128)(2,1)S(1)}, bf16[8,3200]{1,0:T(8,128)(2,1)S(1)}, u32[]{:S(2)}, u32[]{:S(2)}) collective-permute-start(bf16[8,3200]{1,0:T(8,128)(2,1)S(1)} %broadcast_select_fusion.2), channel_id=1, source_target_pairs={{0,256},{256,0},{1,257},{257,1},{2,258},{258,2},{3,259},{259,3},{4... | collective-permute-start | bytes 153608 | tf_op jit(solution)/shard_map/ppermute | solution.py:27
  38.3 5.0 %all-to-all-start.2 = ((bf16[8,8,1280]{2,1,0:T(8,128)(2,1)}), bf16[8,8,1280]{2,1,0:T(8,128)(2,1)S(1)}, u32[]{:S(2)}, u32[]{:S(2)}) async-start(bf16[8,8,1280]{2,1,0:T(8,128)(2,1)} %maximum_bitcast_fusion), calls=%async_computation.2 | async-start | bytes 327680 | tf_op jit(solution)/shard_map/all_to_all | solution.py:23
  43.3 8.3 %all-to-all-done.2 = bf16[8,8,1280]{2,1,0:T(8,128)(2,1)S(1)} async-done(((bf16[8,8,1280]{2,1,0:T(8,128)(2,1)}), bf16[8,8,1280]{2,1,0:T(8,128)(2,1)S(1)}, u32[]{:S(2)}, u32[]{:S(2)}) %all-to-all-start.2) | async-done | bytes 163872 | tf_op jit(solution)/shard_map/all_to_all | solution.py:23
  51.6 0.9 tile.12
  52.5 6.8 %all-to-all-start.1 = ((bf16[8,16,3200]{2,1,0:T(8,128)(2,1)}), bf16[8,16,3200]{2,1,0:T(8,128)(2,1)S(1)}, u32[]{:S(2)}, u32[]{:S(2)}) async-start(bf16[8,16,3200]{2,1,0:T(8,128)(2,1)} %tile.12), calls=%async_computation.1 | async-start | bytes 1638400 | tf_op jit(solution)/shard_map/all_to_all | solution.py:23
  59.4 2.5 %collective-permute-start.3 = (bf16[64,1280]{1,0:T(8,128)(2,1)S(1)}, bf16[64,1280]{1,0:T(8,128)(2,1)S(1)}, u32[]{:S(2)}, u32[]{:S(2)}) collective-permute-start(bf16[64,1280]{1,0:T(8,128)(2,1)S(1)} %bitcast.72), channel_id=1, source_target_pairs={{0,3},{1,2},{2,1},{3,0},{4,7},{5,6},{6,5},{7,4},{8,11},{9,10},{10,... | collective-permute-start | bytes 491528 | tf_op jit(solution)/shard_map/ppermute | solution.py:137
  61.9 3.4 %collective-permute-start.2 = (bf16[64,1280]{1,0:T(8,128)(2,1)S(1)}, bf16[64,1280]{1,0:T(8,128)(2,1)S(1)}, u32[]{:S(2)}, u32[]{:S(2)}) collective-permute-start(bf16[64,1280]{1,0:T(8,128)(2,1)S(1)} %bitcast.73), channel_id=1, source_target_pairs={{0,2},{1,3},{2,0},{3,1},{4,6},{5,7},{6,4},{7,5},{8,10},{9,11},{10,... | collective-permute-start | bytes 491528 | tf_op jit(solution)/shard_map/ppermute | solution.py:137
  65.3 3.1 %collective-permute-start.1 = (bf16[64,1280]{1,0:T(8,128)(2,1)S(1)}, bf16[64,1280]{1,0:T(8,128)(2,1)S(1)}, u32[]{:S(2)}, u32[]{:S(2)}) collective-permute-start(bf16[64,1280]{1,0:T(8,128)(2,1)S(1)} %bitcast.74), channel_id=1, source_target_pairs={{0,1},{1,0},{2,3},{3,2},{4,5},{5,4},{6,7},{7,6},{8,9},{9,8},{10,11... | collective-permute-start | bytes 491528 | tf_op jit(solution)/shard_map/ppermute | solution.py:137
  68.4 1.2 collective-permute-done.2
  69.6 2.1 %collective-permute-done.1 = bf16[64,1280]{1,0:T(8,128)(2,1)S(1)} collective-permute-done((bf16[64,1280]{1,0:T(8,128)(2,1)S(1)}, bf16[64,1280]{1,0:T(8,128)(2,1)S(1)}, u32[]{:S(2)}, u32[]{:S(2)}) %collective-permute-start.1) | collective-permute-done | bytes 163872 | tf_op jit(solution)/shard_map/ppermute | solution.py:137
  71.7 6.6 %collective-permute-start.4 = (bf16[256,1280]{1,0:T(8,128)(2,1)S(1)}, bf16[256,1280]{1,0:T(8,128)(2,1)S(1)}, u32[]{:S(2)}, u32[]{:S(2)}) collective-permute-start(bf16[256,1280]{1,0:T(8,128)(2,1)S(1)} %pad_maximum_fusion), channel_id=1, source_target_pairs={{0,16},{16,0},{1,17},{17,1},{2,18},{18,2},{3,19},{19,3},{4,20},{20... | collective-permute-start | bytes 1966088 | tf_op jit(solution)/shard_map/ppermute | solution.py:27
  78.4 1.5 %collective-permute-done.4 = bf16[256,1280]{1,0:T(8,128)(2,1)S(1)} collective-permute-done((bf16[256,1280]{1,0:T(8,128)(2,1)S(1)}, bf16[256,1280]{1,0:T(8,128)(2,1)S(1)}, u32[]{:S(2)}, u32[]{:S(2)}) %collective-permute-start.4) | collective-permute-done | bytes 655392 | tf_op jit(solution)/shard_map/ppermute | solution.py:27
  81.6 0.8 fusion.15
  82.8 18.5 %all_to_all.57 = bf16[8,144,128]{2,1,0:T(8,128)(2,1)S(1)} all-to-all(bf16[8,144,128]{2,1,0:T(8,128)(2,1)S(1)} %bitcast.70), channel_id=1, replica_groups=mesh['zh'=2,'y'=8,'core'=2,'zl'=4,'x'=4] {'y'}, dimensions={0} | all-to-all | bytes 589824 | tf_op jit(solution)/shard_map/all_to_all | solution.py:23
  101.5 3.2 %collective-permute-start.5 = (bf16[72,2048]{1,0:T(8,128)(2,1)S(1)}, bf16[72,2048]{1,0:T(8,128)(2,1)S(1)}, u32[]{:S(2)}, u32[]{:S(2)}) collective-permute-start(bf16[72,2048]{1,0:T(8,128)(2,1)S(1)} %convolution_convert_fusion), channel_id=1, source_target_pairs={{0,16},{16,0},{1,17},{17,1},{2,18},{18,2},{3,19},{19,3},{4,20},{20... | collective-permute-start | bytes 884744 | tf_op jit(solution)/shard_map/ppermute | solution.py:27
  104.8 1.2 collective-permute-done.5
  106.3 13.4 %all_to_all.58 = bf16[16,72,128]{2,1,0:T(8,128)(2,1)S(1)} all-to-all(bf16[16,72,128]{2,1,0:T(8,128)(2,1)S(1)} %bitcast.71), channel_id=1, replica_groups=mesh['zh'=2,'y'=8,'core'=2,'zl'=4,'x'=4] {'zl','x'}, dimensions={0} | all-to-all | bytes 589824 | tf_op jit(solution)/shard_map/all_to_all | solution.py:23
  119.8 15.9 %all_to_all.59 = bf16[16,72,128]{2,1,0:T(8,128)(2,1)S(1)} all-to-all(bf16[16,72,128]{2,1,0:T(8,128)(2,1)S(1)} %tile.17), channel_id=1, replica_groups=mesh['zh'=2,'y'=8,'core'=2,'zl'=4,'x'=4] {'zh','y'}, dimensions={0} | all-to-all | bytes 589824 | tf_op jit(solution)/shard_map/all_to_all | solution.py:23
  135.7 5.5 %all_gather.7 = bf16[2,1152,128]{2,1,0:T(8,128)(2,1)S(1)} all-gather(bf16[1,1152,128]{2,1,0:T(8,128)(2,1)S(1)} %bitcast.69), channel_id=1, replica_groups=mesh['zh'=2,'y'=8,'core'=2,'zl'=4,'x'=4] {'core'}, dimensions={0}, use_global_device_ids=true | all-gather | bytes 884736 | tf_op jit(solution)/shard_map/all_gather | solution.py:156
  141.4 1.0 copy.20
  142.4 0.9 copy.21
  (48 shorter events, 4.5 us)
Async XLA Ops:
  0.6 12.7 %copy-start = (s32[128]{0:T(128)S(1)}, s32[128]{0:T(128)}, u32[]{:S(2)}) copy-start(s32[128]{0:T(128)} %param.9) | copy-start | bytes 1540
  2.9 26.3 %all-to-all-start = ((bf16[16,8,2560]{2,1,0:T(8,128)(2,1)}), bf16[16,8,2560]{2,1,0:T(8,128)(2,1)S(1)}, u32[]{:S(2)}, u32[]{:S(2)}) async-start(bf16[16,8,2560]{2,1,0:T(8,128)(2,1)} %bitcast.67), calls=%async_computation | async-start | bytes 1310720 | tf_op jit(solution)/shard_map/all_to_all | solution.py:23
  29.6 13.6 %collective-permute-start = (bf16[8,3200]{1,0:T(8,128)(2,1)S(1)}, bf16[8,3200]{1,0:T(8,128)(2,1)S(1)}, u32[]{:S(2)}, u32[]{:S(2)}) collective-permute-start(bf16[8,3200]{1,0:T(8,128)(2,1)S(1)} %broadcast_select_fusion.2), channel_id=1, source_target_pairs={{0,256},{256,0},{1,257},{257,1},{2,258},{258,2},{3,259},{259,3},{4... | collective-permute-start | bytes 153608 | tf_op jit(solution)/shard_map/ppermute | solution.py:27
  38.3 13.3 %all-to-all-start.2 = ((bf16[8,8,1280]{2,1,0:T(8,128)(2,1)}), bf16[8,8,1280]{2,1,0:T(8,128)(2,1)S(1)}, u32[]{:S(2)}, u32[]{:S(2)}) async-start(bf16[8,8,1280]{2,1,0:T(8,128)(2,1)} %maximum_bitcast_fusion), calls=%async_computation.2 | async-start | bytes 327680 | tf_op jit(solution)/shard_map/all_to_all | solution.py:23
  52.5 28.1 %all-to-all-start.1 = ((bf16[8,16,3200]{2,1,0:T(8,128)(2,1)}), bf16[8,16,3200]{2,1,0:T(8,128)(2,1)S(1)}, u32[]{:S(2)}, u32[]{:S(2)}) async-start(bf16[8,16,3200]{2,1,0:T(8,128)(2,1)} %tile.12), calls=%async_computation.1 | async-start | bytes 1638400 | tf_op jit(solution)/shard_map/all_to_all | solution.py:23
  59.4 9.0 %collective-permute-start.3 = (bf16[64,1280]{1,0:T(8,128)(2,1)S(1)}, bf16[64,1280]{1,0:T(8,128)(2,1)S(1)}, u32[]{:S(2)}, u32[]{:S(2)}) collective-permute-start(bf16[64,1280]{1,0:T(8,128)(2,1)S(1)} %bitcast.72), channel_id=1, source_target_pairs={{0,3},{1,2},{2,1},{3,0},{4,7},{5,6},{6,5},{7,4},{8,11},{9,10},{10,... | collective-permute-start | bytes 491528 | tf_op jit(solution)/shard_map/ppermute | solution.py:137
  61.9 7.7 %collective-permute-start.2 = (bf16[64,1280]{1,0:T(8,128)(2,1)S(1)}, bf16[64,1280]{1,0:T(8,128)(2,1)S(1)}, u32[]{:S(2)}, u32[]{:S(2)}) collective-permute-start(bf16[64,1280]{1,0:T(8,128)(2,1)S(1)} %bitcast.73), channel_id=1, source_target_pairs={{0,2},{1,3},{2,0},{3,1},{4,6},{5,7},{6,4},{7,5},{8,10},{9,11},{10,... | collective-permute-start | bytes 491528 | tf_op jit(solution)/shard_map/ppermute | solution.py:137
  65.3 6.4 %collective-permute-start.1 = (bf16[64,1280]{1,0:T(8,128)(2,1)S(1)}, bf16[64,1280]{1,0:T(8,128)(2,1)S(1)}, u32[]{:S(2)}, u32[]{:S(2)}) collective-permute-start(bf16[64,1280]{1,0:T(8,128)(2,1)S(1)} %bitcast.74), channel_id=1, source_target_pairs={{0,1},{1,0},{2,3},{3,2},{4,5},{5,4},{6,7},{7,6},{8,9},{9,8},{10,11... | collective-permute-start | bytes 491528 | tf_op jit(solution)/shard_map/ppermute | solution.py:137
  71.7 8.3 %collective-permute-start.4 = (bf16[256,1280]{1,0:T(8,128)(2,1)S(1)}, bf16[256,1280]{1,0:T(8,128)(2,1)S(1)}, u32[]{:S(2)}, u32[]{:S(2)}) collective-permute-start(bf16[256,1280]{1,0:T(8,128)(2,1)S(1)} %pad_maximum_fusion), channel_id=1, source_target_pairs={{0,16},{16,0},{1,17},{17,1},{2,18},{18,2},{3,19},{19,3},{4,20},{20... | collective-permute-start | bytes 1966088 | tf_op jit(solution)/shard_map/ppermute | solution.py:27
  101.5 4.4 %collective-permute-start.5 = (bf16[72,2048]{1,0:T(8,128)(2,1)S(1)}, bf16[72,2048]{1,0:T(8,128)(2,1)S(1)}, u32[]{:S(2)}, u32[]{:S(2)}) collective-permute-start(bf16[72,2048]{1,0:T(8,128)(2,1)S(1)} %convolution_convert_fusion), channel_id=1, source_target_pairs={{0,16},{16,0},{1,17},{17,1},{2,18},{18,2},{3,19},{19,3},{4,20},{20... | collective-permute-start | bytes 884744 | tf_op jit(solution)/shard_map/ppermute | solution.py:27
